TPU v7x, 256 devices: a whole 4x4x8 slice. The times are simulated.
256 devices in a mesh: modes: 8 (over z_lo, y), space: 32 (over z_hi, x, core).
Axes of the slice: x: 4, y: 4, z: 8 (z_hi: 4, z_lo: 2; z = z_hi * 2 + z_lo), core: 2. Of those that a mesh axis runs over, the one named last changes fastest.
Arguments:
- pressure: float32 [120, 64, 32, 128], P('modes', 'space'), may hold values from -6 to 6
- source: float32 [120, 64, 32, 128], P('modes', 'space'), may hold values from -12 to 12
- perm_modes: float32 [8, 64, 32, 128], P(None, 'space'), may hold values from -3.4 to 3.4, as said below
- triples: int32 [3, 2880], replicated, may hold values from 0 to 119, as said below
- coeffs: float32 [2880], replicated, may hold values from -0.6 to 2, as said below
Outputs:
- applied: float32 [120, 64, 32, 128], P('modes', 'space')
- relaxed: float32 [120, 64, 32, 128], P('modes', 'space')
Inputs may be any that keep to these rules, and one draw needn't show every extreme that they name: `triples`: for each mode i and each k < 8 there are 3 entries with that i and k, in random order; exactly one entry per i has j equal to i, and it has k = 0; k is below 8. `coeffs`: the entry with j equal to i has a coefficient of 0.5 or more. `perm_modes`: the first field is 0.3 or more in every cell.
All inputs are finite; a program needn't handle non-finite values.
Results may differ from a plain program's by a relative error of at most 0.00011.
Values sent between devices are 32-bit elements; how exact they have to be, the bound alone decides.
A program may use at most 128 MiB of HBM per device.

v0:
```python
import jax
import jax.numpy as jnp
from jax import lax
from jax.sharding import PartitionSpec as P

P_SIZE = 120
KA = 8


relax_weight = 0.8


def padded_2(cells, sides, width):
    for axis, dim in sides:
        count = lax.axis_size(axis)
        ends = count - 1
        head = lax.slice_in_dim(cells, 0, width, axis=dim)
        tail = lax.slice_in_dim(cells, cells.shape[dim] - width, cells.shape[dim], axis=dim)
        cells = jnp.concatenate(
            [
                lax.ppermute(tail, axis, [(i, (i + 1) % count) for i in range(ends)]),
                cells,
                lax.ppermute(head, axis, [((i + 1) % count, i) for i in range(ends)]),
            ],
            axis=dim,
        )
    return cells


def coupling_table(triples, coeffs):
    mode_ids = jnp.arange(P_SIZE, dtype=jnp.int32)
    pair_ids = jnp.arange(P_SIZE * KA, dtype=jnp.int32)
    pair_col = triples[1] * KA + triples[2]
    left_hot = (triples[0][:, None] == mode_ids[None, :]).astype(jnp.float32)
    right_hot = (pair_col[:, None] == pair_ids[None, :]).astype(jnp.float32) * coeffs[:, None]
    return jnp.dot(left_hot.T, right_hot, precision=lax.Precision.HIGHEST)


def neighbours(padded):
    middle = padded[..., 1:-1, 1:-1, 1:-1]
    sides = [
        padded[..., 2:, 1:-1, 1:-1],
        padded[..., :-2, 1:-1, 1:-1],
        padded[..., 1:-1, 2:, 1:-1],
        padded[..., 1:-1, :-2, 1:-1],
        padded[..., 1:-1, 1:-1, 2:],
        padded[..., 1:-1, 1:-1, :-2],
    ]
    return (middle, sides)


def apply_fields(perm_ext, field_ext):
    perm_mid, perm_sides = neighbours(perm_ext)
    field_mid, field_sides = neighbours(field_ext)
    running = 0.0
    for perm_side, field_side in zip(perm_sides, field_sides):
        running = running + 0.5 * (perm_mid + perm_side) * (field_mid - field_side)
    return running


def diag_fields(perm_ext):
    perm_mid, perm_sides = neighbours(perm_ext)
    running = 0.0
    for perm_side in perm_sides:
        running = running + 0.5 * (perm_mid + perm_side)
    return running


def pad_inner(field):
    return jnp.pad(field, ((0, 0), (0, 0), (1, 1), (1, 1)))


def field_faces(field):
    extended = padded_2(field, (("space", 1),), 1)
    return pad_inner(extended)


def on_device(pressure, source, perm_modes, triples, coeffs):
    block_shape = pressure.shape
    local_modes = block_shape[0]
    group_count = lax.axis_size("modes")
    block_rows = block_shape[1] * block_shape[2] // group_count
    lane_count = block_shape[3]
    mode_start = lax.axis_index("modes") * local_modes
    coupling_full = coupling_table(triples, coeffs)
    coupling_three = coupling_full.reshape(P_SIZE, P_SIZE, KA)
    perm_ext = pad_inner(padded_2(perm_modes, (("space", 1),), 1))
    pressure_ext = field_faces(pressure)
    stencil_terms = apply_fields(perm_ext, pressure_ext[:, None])
    stencil_terms = stencil_terms.reshape(local_modes, KA, group_count, block_rows, lane_count)
    point_side = lax.all_to_all(stencil_terms, "modes", split_axis=2, concat_axis=0, tiled=True)
    point_side = point_side.reshape(P_SIZE * KA, 1, block_rows, lane_count)
    mixed_sums = jnp.einsum(
        "ab,bxyz->axyz", coupling_full, point_side, precision=lax.Precision.HIGHEST
    )
    applied = lax.all_to_all(mixed_sums, "modes", split_axis=0, concat_axis=1, tiled=True).reshape(
        block_shape
    )
    mode_ids = jnp.arange(P_SIZE, dtype=jnp.int32)
    diag_rows = coupling_three[mode_ids, mode_ids]
    diag_local = lax.dynamic_slice_in_dim(diag_rows, mode_start, local_modes, 0)
    diag_field = diag_fields(perm_ext).reshape(KA, -1)
    scale = jnp.dot(diag_local, diag_field, precision=lax.Precision.HIGHEST).reshape(block_shape)
    relaxed = pressure + relax_weight * (source - applied) / scale
    return (applied, relaxed)


def solution(mesh):
    return jax.shard_map(
        on_device,
        mesh=mesh,
        in_specs=(
            P("modes", "space", None, None),
            P("modes", "space", None, None),
            P(None, "space", None, None),
            P(),
            P(),
        ),
        out_specs=(P("modes", "space", None, None), P("modes", "space", None, None)),
        check_vma=False,
    )
```

profile of v0, /device:TPU:70, one launch (start us, length us, event | category | flops | bytes accessed | tf_op | source)
XLA Modules:
  0.0 102.0 jit_solution(16502163497201895026)
XLA Ops:
  0.6 0.0 copy-start.1
  0.6 1.0 %fusion.35 = (f32[8,1,32,128]{3,2,1,0:T(8,128)S(1)}, f32[8,1,32,128]{3,2,1,0:T(8,128)S(1)}) fusion(f32[8,2,32,128]{3,2,1,0:T(8,128)} %param.7), kind=kLoop, calls=%fused_computation.65 | loop fusion | bytes 524288 | tf_op jit(solution)/shard_map/slice | solution.py:18
  1.7 2.2 %collective-permute-start = (f32[8,1,32,128]{3,2,1,0:T(8,128)S(1)}, f32[8,1,32,128]{3,2,1,0:T(8,128)S(1)}, u32[]{:S(2)}, u32[]{:S(2)}) collective-permute-start(f32[8,1,32,128]{3,2,1,0:T(8,128)S(1)} %get-tuple-element.26), channel_id=1, source_target_pairs={{1,0},{2,1},{3,2},{4,3},{5,4},{6,5},{7,6},{8,7},{9,8},{10,9},{11,1... | collective-permute-start | bytes 393224 | tf_op jit(solution)/shard_map/ppermute | solution.py:23
  3.9 2.2 %collective-permute-start.3 = (f32[8,1,32,128]{3,2,1,0:T(8,128)S(1)}, f32[8,1,32,128]{3,2,1,0:T(8,128)S(1)}, u32[]{:S(2)}, u32[]{:S(2)}) collective-permute-start(f32[8,1,32,128]{3,2,1,0:T(8,128)S(1)} %get-tuple-element.25), channel_id=1, source_target_pairs={{0,1},{1,2},{2,3},{3,4},{4,5},{5,6},{6,7},{7,8},{8,9},{9,10},{10,1... | collective-permute-start | bytes 393224 | tf_op jit(solution)/shard_map/ppermute | solution.py:21
  6.0 1.1 %fusion.34 = (f32[15,1,32,128]{3,2,1,0:T(8,128)S(1)}, f32[15,1,32,128]{3,2,1,0:T(8,128)S(1)}) fusion(f32[15,2,32,128]{3,2,1,0:T(8,128)} %param.5), kind=kLoop, calls=%fused_computation.64 | loop fusion | bytes 983040 | tf_op jit(solution)/shard_map/slice | solution.py:18
  7.1 7.2 %collective-permute-start.1 = (f32[15,1,32,128]{3,2,1,0:T(8,128)S(1)}, f32[15,1,32,128]{3,2,1,0:T(8,128)S(1)}, u32[]{:S(2)}, u32[]{:S(2)}) collective-permute-start(f32[15,1,32,128]{3,2,1,0:T(8,128)S(1)} %get-tuple-element.23), channel_id=1, source_target_pairs={{0,1},{1,2},{2,3},{3,4},{4,5},{5,6},{6,7},{7,8},{8,9},{9,10},{10,1... | collective-permute-start | bytes 737288 | tf_op jit(solution)/shard_map/ppermute | solution.py:21
  14.3 1.9 %collective-permute-start.2 = (f32[15,1,32,128]{3,2,1,0:T(8,128)S(1)}, f32[15,1,32,128]{3,2,1,0:T(8,128)S(1)}, u32[]{:S(2)}, u32[]{:S(2)}) collective-permute-start(f32[15,1,32,128]{3,2,1,0:T(8,128)S(1)} %get-tuple-element.24), channel_id=1, source_target_pairs={{1,0},{2,1},{3,2},{4,3},{5,4},{6,5},{7,6},{8,7},{9,8},{10,9},{11,1... | collective-permute-start | bytes 737288 | tf_op jit(solution)/shard_map/ppermute | solution.py:23
  16.3 0.0 collective-permute-done
  16.3 0.0 collective-permute-done.3
  16.3 1.4 %select_maximum_fusion.2 = f32[8,4,34,130]{3,2,1,0:T(8,128)S(1)} fusion(f32[8,1,32,128]{3,2,1,0:T(8,128)S(1)} %collective-permute-done, f32[8,2,32,128]{3,2,1,0:T(8,128)} %param.7, f32[8,1,32,128]{3,2,1,0:T(8,128)S(1)} %collective-permute-done.3), kind=kLoop, calls=%fused_computation.23 | loop fusion | flops 2121600 | bytes 1090048 | tf_op jit(solution)/shard_map/concatenate | solution.py:19
  17.7 0.0 copy-done.1
  17.7 0.0 copy-start
  17.7 0.3 add_add_fusion
  18.0 0.2 copy.46
  18.2 0.2 copy.48
  18.3 0.2 copy.50
  18.5 0.2 copy.52
  18.7 0.2 copy.54
  18.8 0.2 copy.56
  19.0 0.0 collective-permute-done.1
  19.0 0.9 collective-permute-done.2
  20.0 0.0 copy-done
  20.0 0.7 fusion.5
  20.7 0.8 slice_subtract_fusion.5
  21.5 0.3 copy.47
  21.8 0.3 copy.49
  22.1 0.3 copy.51
  22.4 0.3 copy.53
  22.7 0.3 copy.55
  23.0 0.3 copy.57
  23.3 4.1 %multiply_add_fusion = f32[15,8,8,8,128]{4,1,0,3,2:T(8,128)} fusion(f32[15,8,8,128]{3,0,2,1:T(8,128)S(1)} %copy.57, f32[8,8,8,128]{3,0,2,1:T(8,128)S(1)} %copy.56, f32[15,8,8,128]{3,0,2,1:T(8,128)S(1)} %copy.55, f32[8,8,8,128]{3,0,2,1:T(8,128)S(1)} %copy.54, f32[15,8,8,128]{3,0,2,1:T(8,128)S(1)} %copy.53, f32[8,8,8,128]{3,0,2,1:T(8,128)S(1)} %copy.52, ...), kind=kLoop, calls=%fused_computation.7 | loop fusion | flops 10813440 | bytes 8454144 | tf_op jit(solution)/shard_map/add | solution.py:57
  27.3 0.0 copy-start.3
  27.3 0.0 copy-start.4
  27.3 6.0 %all-to-all-start = ((f32[15,8,8,8,128]{4,1,0,3,2:T(8,128)}), f32[15,8,8,8,128]{4,1,0,3,2:T(8,128)}, u32[]{:S(2)}, u32[]{:S(2)}) async-start(f32[15,8,8,8,128]{4,1,0,3,2:T(8,128)} %multiply_add_fusion), calls=%async_computation | async-start | bytes 7864320 | tf_op jit(solution)/shard_map/all_to_all | solution.py:91
  33.3 0.0 copy-done.3
  33.3 0.1 slice_reduce_fusion
  33.4 0.0 copy-done.4
  33.4 5.9 %fusion = f32[120,960]{1,0:T(8,128)S(1)} fusion(f32[2880]{0:T(1024)S(1)} %copy-done.4, s32[2880]{0:T(1024)S(1)} %get-tuple-element.9, s32[2880]{0:T(1024)S(1)} %get-tuple-element.8), kind=kOutput, calls=%fused_computation.1 | convolution fusion | flops 3987187200 | bytes 495360 | tf_op jit(solution)/shard_map/dot_general | solution.py:36
  39.3 39.8 %all-to-all-done = f32[15,8,8,8,128]{4,1,0,3,2:T(8,128)} async-done(((f32[15,8,8,8,128]{4,1,0,3,2:T(8,128)}), f32[15,8,8,8,128]{4,1,0,3,2:T(8,128)}, u32[]{:S(2)}, u32[]{:S(2)}) %all-to-all-start) | async-done | bytes 3932192 | tf_op jit(solution)/shard_map/all_to_all | solution.py:91
  79.1 2.4 %copy.58 = f32[8,15,8,1,8,128]{5,2,1,0,4,3:T(8,128)S(1)} copy(f32[8,15,8,1,8,128]{5,2,1,4,0,3:T(8,128)} %bitcast.15) | data formatting | bytes 7864320 | tf_op jit(solution)/shard_map/all_to_all | solution.py:91
  81.5 2.3 %convolution_bitcast_fusion = f32[120,1,8,128]{3,0,2,1:T(8,128)S(1)} fusion(f32[960,8,128]{2,0,1:T(8,128)S(1)} %bitcast.46, f32[120,960]{1,0:T(8,128)S(1)} %fusion), kind=kOutput, calls=%fused_computation.30 | convolution fusion | flops 1415577600 | bytes 4884480 | tf_op jit(solution)/shard_map/ab,bxyz->axyz/dot_general | solution.py:93
  83.8 0.9 copy.59
  84.7 4.9 %all-to-all-start.1 = ((f32[120,1,8,128]{3,2,1,0:T(8,128)}), f32[120,1,8,128]{3,2,1,0:T(8,128)S(1)}, u32[]{:S(2)}, u32[]{:S(2)}) async-start(f32[120,1,8,128]{3,2,1,0:T(8,128)} %copy.59), calls=%async_computation.1 | async-start | bytes 983040 | tf_op jit(solution)/shard_map/all_to_all | solution.py:96
  89.6 0.2 copy.62
  89.8 4.5 %copy.63 = f32[120,120,8]{2,1,0:T(8,128)} copy(f32[120,120,8]{0,2,1:T(8,128)S(1)} %bitcast.56) | data formatting | bytes 921600 | tf_op jit(solution)/shard_map/reshape | solution.py:86
  94.2 0.0 copy-start.2
  94.3 2.1 %gather_fusion = f32[120,8]{1,0:T(8,128)S(1)} fusion(f32[120,120,8]{2,1,0:T(8,128)} %copy.63, s32[120]{0:T(128)S(1)} %or_bitcast_fusion), kind=kCustom, calls=%fused_computation | custom fusion | bytes 8640 | tf_op jit(solution)/shard_map/gather | solution.py:100
  96.4 0.2 copy.78
  96.6 2.4 %all-to-all-done.1 = f32[120,1,8,128]{3,2,1,0:T(8,128)S(1)} async-done(((f32[120,1,8,128]{3,2,1,0:T(8,128)}), f32[120,1,8,128]{3,2,1,0:T(8,128)S(1)}, u32[]{:S(2)}, u32[]{:S(2)}) %all-to-all-start.1) | async-done | bytes 491552 | tf_op jit(solution)/shard_map/all_to_all | solution.py:96
  99.0 0.1 copy.60
  99.1 0.9 copy.66
  100.0 0.0 copy-done.2
  100.0 1.1 %fusion.12 = f32[15,2,32,128]{3,0,2,1:T(8,128)S(1)} fusion(f32[2,32,128,8]{2,3,1,0:T(8,128)S(1)} %bitcast.63, f32[15,2,32,128]{3,2,1,0:T(8,128)S(1)} %copy-done, f32[15,2,32,128]{3,0,2,1:T(8,128)S(1)} %bitcast.48, f32[15,2,32,128]{3,2,1,0:T(8,128)S(1)} %copy-done.2, f32[120,8]{1,0:T(8,128)S(1)} %gather_fusion, s32[]{:T(128)S(6)} %select_n.2), kind=kOutput, calls=%fused_computation.29 | convolution fusion | flops 12288000 | bytes 2269188 | tf_op jit(solution)/shard_map/dot_general | solution.py:103
  101.1 0.9 copy.67
  (1 shorter events, 0.0 us)
Async XLA Ops:
  0.6 17.0 %copy-start.1 = (f32[8,2,32,128]{3,2,1,0:T(8,128)S(1)}, f32[8,2,32,128]{3,2,1,0:T(8,128)}, u32[]{:S(2)}) copy-start(f32[8,2,32,128]{3,2,1,0:T(8,128)} %param.7) | copy-start | bytes 786436
  1.7 14.6 %collective-permute-start = (f32[8,1,32,128]{3,2,1,0:T(8,128)S(1)}, f32[8,1,32,128]{3,2,1,0:T(8,128)S(1)}, u32[]{:S(2)}, u32[]{:S(2)}) collective-permute-start(f32[8,1,32,128]{3,2,1,0:T(8,128)S(1)} %get-tuple-element.26), channel_id=1, source_target_pairs={{1,0},{2,1},{3,2},{4,3},{5,4},{6,5},{7,6},{8,7},{9,8},{10,9},{11,1... | collective-permute-start | bytes 393224 | tf_op jit(solution)/shard_map/ppermute | solution.py:23
  3.9 12.4 %collective-permute-start.3 = (f32[8,1,32,128]{3,2,1,0:T(8,128)S(1)}, f32[8,1,32,128]{3,2,1,0:T(8,128)S(1)}, u32[]{:S(2)}, u32[]{:S(2)}) collective-permute-start(f32[8,1,32,128]{3,2,1,0:T(8,128)S(1)} %get-tuple-element.25), channel_id=1, source_target_pairs={{0,1},{1,2},{2,3},{3,4},{4,5},{5,6},{6,7},{7,8},{8,9},{9,10},{10,1... | collective-permute-start | bytes 393224 | tf_op jit(solution)/shard_map/ppermute | solution.py:21
  7.1 11.9 %collective-permute-start.1 = (f32[15,1,32,128]{3,2,1,0:T(8,128)S(1)}, f32[15,1,32,128]{3,2,1,0:T(8,128)S(1)}, u32[]{:S(2)}, u32[]{:S(2)}) collective-permute-start(f32[15,1,32,128]{3,2,1,0:T(8,128)S(1)} %get-tuple-element.23), channel_id=1, source_target_pairs={{0,1},{1,2},{2,3},{3,4},{4,5},{5,6},{6,7},{7,8},{8,9},{9,10},{10,1... | collective-permute-start | bytes 737288 | tf_op jit(solution)/shard_map/ppermute | solution.py:21
  14.3 5.6 %collective-permute-start.2 = (f32[15,1,32,128]{3,2,1,0:T(8,128)S(1)}, f32[15,1,32,128]{3,2,1,0:T(8,128)S(1)}, u32[]{:S(2)}, u32[]{:S(2)}) collective-permute-start(f32[15,1,32,128]{3,2,1,0:T(8,128)S(1)} %get-tuple-element.24), channel_id=1, source_target_pairs={{1,0},{2,1},{3,2},{4,3},{5,4},{6,5},{7,6},{8,7},{9,8},{10,9},{11,1... | collective-permute-start | bytes 737288 | tf_op jit(solution)/shard_map/ppermute | solution.py:23
  17.7 2.3 %copy-start = (f32[15,2,32,128]{3,2,1,0:T(8,128)S(1)}, f32[15,2,32,128]{3,2,1,0:T(8,128)}, u32[]{:S(2)}) copy-start(f32[15,2,32,128]{3,2,1,0:T(8,128)} %param.5) | copy-start | bytes 1474564
  27.3 6.0 %copy-start.3 = (s32[3,2880]{1,0:T(4,128)S(1)}, s32[3,2880]{1,0:T(4,128)}, u32[]{:S(2)}) copy-start(s32[3,2880]{1,0:T(4,128)} %param.8) | copy-start | bytes 103684
  27.3 6.0 %copy-start.4 = (f32[2880]{0:T(1024)S(1)}, f32[2880]{0:T(1024)}, u32[]{:S(2)}) copy-start(f32[2880]{0:T(1024)} %param.9) | copy-start | bytes 34564
  27.3 51.8 %all-to-all-start = ((f32[15,8,8,8,128]{4,1,0,3,2:T(8,128)}), f32[15,8,8,8,128]{4,1,0,3,2:T(8,128)}, u32[]{:S(2)}, u32[]{:S(2)}) async-start(f32[15,8,8,8,128]{4,1,0,3,2:T(8,128)} %multiply_add_fusion), calls=%async_computation | async-start | bytes 7864320 | tf_op jit(solution)/shard_map/all_to_all | solution.py:91
  84.7 14.3 %all-to-all-start.1 = ((f32[120,1,8,128]{3,2,1,0:T(8,128)}), f32[120,1,8,128]{3,2,1,0:T(8,128)S(1)}, u32[]{:S(2)}, u32[]{:S(2)}) async-start(f32[120,1,8,128]{3,2,1,0:T(8,128)} %copy.59), calls=%async_computation.1 | async-start | bytes 983040 | tf_op jit(solution)/shard_map/all_to_all | solution.py:96
  94.2 5.8 %copy-start.2 = (f32[15,2,32,128]{3,2,1,0:T(8,128)S(1)}, f32[15,2,32,128]{3,2,1,0:T(8,128)}, u32[]{:S(2)}) copy-start(f32[15,2,32,128]{3,2,1,0:T(8,128)} %param.6) | copy-start | bytes 1474564
where the time goes:
time: 103 us; the launch traced here: 102 us
  waiting for transfers between devices  43.2 us (42%)
  starting transfers between devices  24.3 us (24%)
  local copies, waits for them, and re-layouts  17 us (17%)
  matrix products  9.21 us (9%)
  other arithmetic  7.37 us (7%)
    all_to_all x1, waiting for transfers between devices, on_device(): lax.all_to_all(stencil_terms, 'modes', split_axis=2, concat_axis=0, tiled...  39.8 us
    ppermute x2, starting transfers between devices, padded_2(): lax.ppermute(tail, axis, [(i, (i + 1) % count) for i in range(ends)])  9.35 us
    all_to_all x1, starting transfers between devices, on_device(): lax.all_to_all(stencil_terms, 'modes', split_axis=2, concat_axis=0, tiled...  5.96 us
    dot_general x1, matrix products, coupling_table(): return jnp.dot(left_hot.T, right_hot, precision=lax.Precision.HIGHEST)  5.86 us
    all_to_all x1, starting transfers between devices, on_device(): lax.all_to_all(mixed_sums, 'modes', split_axis=0, concat_axis=1, tiled=True)  4.89 us
    reshape x1, local copies, waits for them, and re-layouts, on_device(): coupling_three = coupling_full.reshape(P_SIZE, P_SIZE, KA)  4.47 us
    ppermute x2, starting transfers between devices, padded_2(): lax.ppermute(head, axis, [((i + 1) % count, i) for i in range(ends)])  4.1 us
    add x1, other arithmetic, apply_fields(): running = running + 0.5 * (perm_mid + perm_side) * (field_mid - field_side)  4.05 us
  transfers between devices with their start and end apart: 6, of which 3 were waited for; matrix products, arithmetic and copies ran while one was open for 16% of the time, Pallas kernels for 0%

commit v1 on v0

v1 whole, which is shorter than its diff:
```python
import functools

import jax
import jax.numpy as jnp
from jax import lax
from jax.experimental import pallas as pl
from jax.experimental.pallas import tpu as pltpu
from jax.sharding import PartitionSpec as P

KA = 8
GROUPS = 8
LOCAL = 15
PAD = 16
LAYERS = 2
ROWS = 32
LANES = 128
OWN = ROWS // GROUPS
ENTRIES = 2880
WIDE = GROUPS * PAD
relax_weight = 0.8

MESH = pl.DeviceIdType.MESH
F32 = jnp.float32
BF16 = jnp.bfloat16


def kernel(
    space_count,
    p_hbm,
    s_hbm,
    a_hbm,
    tri_hbm,
    cf_hbm,
    out_a_hbm,
    out_r_hbm,
    p_v,
    s_v,
    a_v,
    tri_v,
    cf_v,
    t,
    q,
    r_out,
    ret,
    w_mat,
    a_hot,
    m_buf,
    w_f,
    dg,
    cdb,
    inv_v,
    base_v,
    oa_v,
    or_v,
    in_sem,
    out_sem,
    a2a_send,
    a2a_recv,
    low_send,
    low_recv,
    high_send,
    high_recv,
    perm_send,
    perm_recv,
    ret_send,
    ret_recv,
):
    m = lax.axis_index("modes")
    s = lax.axis_index("space")
    s_up = lax.rem(s + 1, space_count)
    s_dn = lax.rem(s + space_count - 1, space_count)

    def peer_to(d):
        return lax.rem(m + d, GROUPS)

    def peer_from(d):
        return lax.rem(m + GROUPS - d, GROUPS)

    def mode_rows(g):
        return pl.ds(pl.multiple_of(g * PAD, PAD), PAD)

    barrier = pltpu.get_barrier_semaphore()
    for d in range(1, GROUPS):
        pl.semaphore_signal(barrier, inc=1, device_id=(peer_to(d), s), device_id_type=MESH)
    for side in (s_up, s_dn):
        pl.semaphore_signal(barrier, inc=1, device_id=(m, side), device_id_type=MESH)

    load_p = pltpu.make_async_copy(p_hbm, p_v.at[0 : LOCAL * 64], in_sem.at[0])
    load_a = pltpu.make_async_copy(a_hbm, a_v.at[:, 1:3], in_sem.at[1])
    load_t = pltpu.make_async_copy(tri_hbm, tri_v, in_sem.at[2])
    load_c = pltpu.make_async_copy(cf_hbm, cf_v, in_sem.at[3])
    load_s = pltpu.make_async_copy(s_hbm, s_v, in_sem.at[4])
    for load in (load_p, load_a, load_t, load_c, load_s):
        load.start()

    p_v[LOCAL * 64 :, :] = jnp.zeros((64, LANES), F32)
    t[:, 0] = jnp.zeros((LAYERS, PAD, LANES), F32)
    t[:, ROWS + 1] = jnp.zeros((LAYERS, PAD, LANES), F32)
    r_out[...] = jnp.zeros(r_out.shape, F32)
    load_p.wait()

    def stage(row, carry):
        for layer in range(LAYERS):
            for half in range(2):
                start = half * 8 * 64 + layer * ROWS + row
                t[layer, row + 1, half * 8 : half * 8 + 8, :] = p_v[pl.ds(start, 8, stride=64), :]
        return carry

    lax.fori_loop(0, ROWS, stage, 0)
    q[1:3, :, mode_rows(m), :] = t[:, pl.ds(m * OWN, OWN + 2), :, :]

    def send_block(d):
        g = peer_to(d)
        return pltpu.make_async_remote_copy(
            src_ref=t.at[:, pl.ds(g * OWN, OWN + 2)],
            dst_ref=q.at[1:3, :, mode_rows(m), :],
            send_sem=a2a_send.at[d],
            recv_sem=a2a_recv.at[d],
            device_id=(g, s),
            device_id_type=MESH,
        )

    def halo(d, up):
        rows = mode_rows(peer_from(d))
        sems = (high_send, high_recv) if up else (low_send, low_recv)
        return pltpu.make_async_remote_copy(
            src_ref=q.at[2 if up else 1, 1 : OWN + 1, rows, :],
            dst_ref=q.at[0 if up else 3, 1 : OWN + 1, rows, :],
            send_sem=sems[0].at[d],
            recv_sem=sems[1].at[d],
            device_id=(m, s_up if up else s_dn),
            device_id_type=MESH,
        )

    def perm_halo(up):
        return pltpu.make_async_remote_copy(
            src_ref=a_v.at[:, 2 if up else 1],
            dst_ref=a_v.at[:, 0 if up else 3],
            send_sem=perm_send.at[1 if up else 0],
            recv_sem=perm_recv.at[1 if up else 0],
            device_id=(m, s_up if up else s_dn),
            device_id_type=MESH,
        )

    def send_back(d):
        g = peer_to(d)
        return pltpu.make_async_remote_copy(
            src_ref=r_out.at[g],
            dst_ref=ret.at[:, pl.ds(pl.multiple_of(m * OWN * PAD, OWN * PAD), OWN * PAD), :],
            send_sem=ret_send.at[d],
            recv_sem=ret_recv.at[d],
            device_id=(g, s),
            device_id_type=MESH,
        )

    pl.semaphore_wait(barrier, GROUPS - 1 + 2)
    for d in range(1, GROUPS):
        send_block(d).start()
    load_a.wait()
    perm_halo(True).start()
    perm_halo(False).start()
    halo(0, True).start()
    halo(0, False).start()

    load_t.wait()
    load_c.wait()
    mode_i = tri_v[0:1, :]
    mode_j = tri_v[1:2, :]
    mode_k = tri_v[2:3, :]
    row_i = mode_i + ((mode_i * 274) >> 12)
    col_jk = mode_j + 113 * ((mode_j * 274) >> 12) + PAD * mode_k
    cf = cf_v[...].reshape(1, ENTRIES)
    cf_hi = cf.astype(BF16).astype(F32)
    cf_lo = cf - cf_hi
    is_row = lax.broadcasted_iota(jnp.int32, (WIDE, ENTRIES), 0) == row_i
    a_hot[0:WIDE, :] = jnp.where(is_row, cf_hi, 0.0).astype(BF16)
    a_hot[WIDE:, :] = jnp.where(is_row, cf_lo, 0.0).astype(BF16)

    def table(c, carry):
        cols = lax.broadcasted_iota(jnp.int32, (2 * WIDE, ENTRIES), 0) + c * (2 * WIDE)
        b_hot = jnp.where(cols == col_jk, 1.0, 0.0).astype(BF16)
        both = lax.dot_general(
            a_hot[...], b_hot, (((1,), (1,)), ((), ())), preferred_element_type=F32
        )
        coupled = both[:WIDE] + both[WIDE:]
        for part in range(2):
            one = coupled[:, part * WIDE : (part + 1) * WIDE]
            hi = one.astype(BF16)
            lo = (one - hi.astype(F32)).astype(BF16)
            for side in range(2):
                w_mat[2 * c + part, 0:WIDE, side * WIDE : (side + 1) * WIDE] = hi
                w_mat[2 * c + part, WIDE:, side * WIDE : (side + 1) * WIDE] = lo
        return carry

    lax.fori_loop(0, GROUPS // 2, table, 0)

    perm_halo(True).wait_recv()
    perm_halo(False).wait_recv()
    has_dn = (s > 0).astype(F32)
    has_up = (s < space_count - 1).astype(F32)
    row_ids = lax.broadcasted_iota(jnp.int32, (ROWS, LANES), 0)
    lane_ids = lax.broadcasted_iota(jnp.int32, (ROWS, LANES), 1)

    def weights(k, carry):
        for layer in range(LAYERS):
            a = a_v[k, layer + 1]
            low = a_v[k, layer]
            high = a_v[k, layer + 2]
            if layer == 0:
                low = low * has_dn
            else:
                high = high * has_up
            sides = (
                low,
                high,
                jnp.where(row_ids > 0, pltpu.roll(a, 1, 0), 0.0),
                jnp.where(row_ids < ROWS - 1, pltpu.roll(a, ROWS - 1, 0), 0.0),
                jnp.where(lane_ids > 0, pltpu.roll(a, 1, 1), 0.0),
                jnp.where(lane_ids < LANES - 1, pltpu.roll(a, LANES - 1, 1), 0.0),
            )
            total = jnp.zeros((ROWS, LANES), F32)
            for f, side in enumerate(sides):
                w = 0.5 * (a + side)
                w_f[f, k, layer] = w
                total = total + w
            dg[k, layer] = total
        return carry

    lax.fori_loop(0, KA, weights, 0)

    def chunk(d):
        g = peer_from(d)
        rows = mode_rows(g)
        lanes = lax.broadcasted_iota(jnp.int32, (PAD, LANES), 1)
        for layer in range(LAYERS):
            for r in range(OWN):
                p = q[layer + 1, r + 1, rows, :]
                low = q[layer, r + 1, rows, :]
                high = q[layer + 2, r + 1, rows, :]
                if layer == 0:
                    low = low * has_dn
                else:
                    high = high * has_up
                diffs = (
                    p - low,
                    p - high,
                    p - q[layer + 1, r, rows, :],
                    p - q[layer + 1, r + 2, rows, :],
                    p - jnp.where(lanes > 0, pltpu.roll(p, 1, 1), 0.0),
                    p - jnp.where(lanes < LANES - 1, pltpu.roll(p, LANES - 1, 1), 0.0),
                )
                at = (layer * OWN + r) * LANES
                for k in range(KA):
                    total = None
                    for f in range(6):
                        term = w_f[f, k, layer, pl.ds(m * OWN + r, 1), :] * diffs[f]
                        total = term if total is None else total + term
                    hi = total.astype(BF16)
                    lo = (total - hi.astype(F32)).astype(BF16)
                    m_buf[k * PAD : (k + 1) * PAD, at : at + LANES] = hi
                    m_buf[WIDE + k * PAD : WIDE + (k + 1) * PAD, at : at + LANES] = lo
            for n in range(OWN // 2):
                at = (layer * OWN + 2 * n) * LANES
                prod = jnp.dot(
                    w_mat[g], m_buf[:, at : at + 2 * LANES], preferred_element_type=F32
                )
                prod = prod[:WIDE] + prod[WIDE:]
                for part in range(2):
                    r = 2 * n + part
                    for go in range(GROUPS):
                        r_out[go, layer, r * PAD : (r + 1) * PAD, :] += prod[
                            go * PAD : (go + 1) * PAD, part * LANES : (part + 1) * LANES
                        ]

    def step(d, carry):
        @pl.when(d < GROUPS)
        def _():
            send_block(d).wait_recv()
            halo(d, True).start()
            halo(d, False).start()

        halo(d - 1, True).wait_recv()
        halo(d - 1, False).wait_recv()
        chunk(d - 1)
        return carry

    lax.fori_loop(1, GROUPS + 1, step, 0)

    for d in range(1, GROUPS):
        send_back(d).start()
    ret[:, pl.ds(pl.multiple_of(m * OWN * PAD, OWN * PAD), OWN * PAD), :] = r_out[m]

    own_rows = w_mat[m, mode_rows(m), 0:WIDE].astype(F32) + w_mat[
        m, pl.ds(pl.multiple_of(WIDE + m * PAD, PAD), PAD), 0:WIDE
    ].astype(F32)
    sub = lax.broadcasted_iota(jnp.int32, (PAD, LANES), 0)
    lane = lax.broadcasted_iota(jnp.int32, (PAD, LANES), 1)
    for k in range(KA):
        picked = jnp.where(lane == sub + k * PAD, own_rows, 0.0)
        cdb[k] = jnp.broadcast_to(jnp.sum(picked, axis=1, keepdims=True), (PAD, LANES))

    load_s.wait()

    def scales(j, carry):
        for layer in range(LAYERS):
            scale = jnp.zeros((ROWS, LANES), F32)
            for k in range(KA):
                scale = scale + cdb[k, pl.ds(j, 1), :] * dg[k, layer]
            at = pl.ds(pl.multiple_of(j * 64 + layer * ROWS, ROWS), ROWS)
            inv = relax_weight / scale
            inv_v[at, :] = inv
            base_v[at, :] = p_v[at, :] + s_v[at, :] * inv
        return carry

    lax.fori_loop(0, LOCAL, scales, 0)

    for d in range(1, GROUPS):
        send_back(d).wait_recv()

    def finish(j, carry):
        for layer in range(LAYERS):
            for r8 in range(ROWS // 8):
                got = ret[layer, pl.ds(r8 * 8 * PAD + j, 8, stride=PAD), :]
                at = pl.ds(pl.multiple_of(j * 64 + layer * ROWS + r8 * 8, 8), 8)
                oa_v[at, :] = got
                or_v[at, :] = base_v[at, :] - got * inv_v[at, :]
        return carry

    lax.fori_loop(0, LOCAL, finish, 0)
    out_a = pltpu.make_async_copy(oa_v, out_a_hbm, out_sem.at[0])
    out_r = pltpu.make_async_copy(or_v, out_r_hbm, out_sem.at[1])
    out_a.start()
    out_r.start()

    for d in range(1, GROUPS):
        send_block(d).wait_send()
        send_back(d).wait_send()
    for d in range(GROUPS):
        halo(d, True).wait_send()
        halo(d, False).wait_send()
    perm_halo(True).wait_send()
    perm_halo(False).wait_send()
    out_a.wait()
    out_r.wait()


def solution(mesh):
    space_count = mesh.shape["space"]
    cells = (LOCAL * LAYERS * ROWS, LANES)

    def on_device(pressure, source, perm_modes, triples, coeffs):
        applied, relaxed = pl.pallas_call(
            functools.partial(kernel, space_count),
            out_shape=[jax.ShapeDtypeStruct(cells, F32)] * 2,
            in_specs=[pl.BlockSpec(memory_space=pl.ANY)] * 5,
            out_specs=[pl.BlockSpec(memory_space=pl.ANY)] * 2,
            scratch_shapes=[
                pltpu.VMEM((PAD * LAYERS * ROWS, LANES), F32),
                pltpu.VMEM(cells, F32),
                pltpu.VMEM((KA, LAYERS + 2, ROWS, LANES), F32),
                pltpu.VMEM((3, ENTRIES), jnp.int32),
                pltpu.VMEM((ENTRIES,), F32),
                pltpu.VMEM((LAYERS, ROWS + 2, PAD, LANES), F32),
                pltpu.VMEM((LAYERS + 2, OWN + 2, WIDE, LANES), F32),
                pltpu.VMEM((GROUPS, LAYERS, OWN * PAD, LANES), F32),
                pltpu.VMEM((LAYERS, ROWS * PAD, LANES), F32),
                pltpu.VMEM((GROUPS, 2 * WIDE, 2 * WIDE), BF16),
                pltpu.VMEM((2 * WIDE, ENTRIES), BF16),
                pltpu.VMEM((2 * WIDE, LAYERS * OWN * LANES), BF16),
                pltpu.VMEM((6, KA, LAYERS, ROWS, LANES), F32),
                pltpu.VMEM((KA, LAYERS, ROWS, LANES), F32),
                pltpu.VMEM((KA, PAD, LANES), F32),
                pltpu.VMEM(cells, F32),
                pltpu.VMEM(cells, F32),
                pltpu.VMEM(cells, F32),
                pltpu.VMEM(cells, F32),
                pltpu.SemaphoreType.DMA((5,)),
                pltpu.SemaphoreType.DMA((2,)),
            ]
            + [pltpu.SemaphoreType.DMA((GROUPS,))] * 6
            + [pltpu.SemaphoreType.DMA((2,))] * 2
            + [pltpu.SemaphoreType.DMA((GROUPS,))] * 2,
            compiler_params=pltpu.CompilerParams(
                collective_id=0, has_side_effects=True, vmem_limit_bytes=48 * 1024 * 1024
            ),
        )(
            pressure.reshape(cells),
            source.reshape(cells),
            perm_modes,
            triples,
            coeffs,
        )
        return applied.reshape(pressure.shape), relaxed.reshape(pressure.shape)

    return jax.shard_map(
        on_device,
        mesh=mesh,
        in_specs=(
            P("modes", "space", None, None),
            P("modes", "space", None, None),
            P(None, "space", None, None),
            P(),
            P(),
        ),
        out_specs=(P("modes", "space", None, None), P("modes", "space", None, None)),
        check_vma=False,
    )
```

time: 103 us -> 59.9 us (0.58)
  the two profiles are of different devices: /device:TPU:70 before, /device:TPU:56 now
where the time goes in v1:
time: 59.9 us; the launch traced here: 59.6 us
  Pallas kernels  52.9 us (88%)
  local copies, waits for them, and re-layouts  6.06 us (10%)
  between operations  0.65 us (1%)
    pallas_call x1, Pallas kernels, on_device(): pl.pallas_call(functools.partial(kernel, space_count), out_shape=[jax.Sha...  52.9 us
    unnamed x12, local copies, waits for them, and re-layouts  6.06 us

profile of v1, /device:TPU:56, one launch (start us, length us, event | category | flops | bytes accessed | tf_op | source)
XLA Modules:
  0.0 59.6 jit_solution(592110680378714403)
XLA Ops:
  0.6 0.0 copy-start
  0.6 1.0 %copy-done = f32[15,2,32,128]{3,2,1,0:T(8,128)S(1)} copy-done((f32[15,2,32,128]{3,2,1,0:T(8,128)S(1)}, f32[15,2,32,128]{3,2,1,0:T(8,128)}, u32[]{:S(2)}) %copy-start) | copy-done | bytes 491544
  1.7 0.0 copy-start.1
  1.7 1.0 %copy-done.1 = f32[15,2,32,128]{3,2,1,0:T(8,128)S(1)} copy-done((f32[15,2,32,128]{3,2,1,0:T(8,128)S(1)}, f32[15,2,32,128]{3,2,1,0:T(8,128)}, u32[]{:S(2)}) %copy-start.1) | copy-done | bytes 491544
  2.7 0.0 copy-start.2
  2.7 0.9 %copy-done.2 = f32[8,2,32,128]{3,2,1,0:T(8,128)S(1)} copy-done((f32[8,2,32,128]{3,2,1,0:T(8,128)S(1)}, f32[8,2,32,128]{3,2,1,0:T(8,128)}, u32[]{:S(2)}) %copy-start.2) | copy-done | bytes 262168
  3.6 0.0 copy-start.3
  3.6 0.8 %copy-done.3 = s32[3,2880]{1,0:T(4,128)S(1)} copy-done((s32[3,2880]{1,0:T(4,128)S(1)}, s32[3,2880]{1,0:T(4,128)}, u32[]{:S(2)}) %copy-start.3) | copy-done | bytes 34584
  4.4 0.0 copy-start.4
  4.4 0.7 %copy-done.4 = f32[2880]{0:T(1024)S(1)} copy-done((f32[2880]{0:T(1024)S(1)}, f32[2880]{0:T(1024)}, u32[]{:S(2)}) %copy-start.4) | copy-done | bytes 11544
  5.1 52.9 %shard_map.68 = (f32[960,128]{1,0:T(8,128)S(1)}, f32[960,128]{1,0:T(8,128)S(1)}) custom-call(f32[960,128]{1,0:T(8,128)S(1)} %bitcast.4, f32[960,128]{1,0:T(8,128)S(1)} %bitcast.5, f32[8,2,32,128]{3,2,1,0:T(8,128)S(1)} %copy-done.2, s32[3,2880]{1,0:T(4,128)S(1)} %copy-done.3, f32[2880]{0:T(1024)S(1)} %copy-done.4), custom_call_target="tpu_custom_call" | custom-call | tf_op jit(solution)/shard_map/pallas_call | solution.py:352
  58.0 0.8 %copy.9 = f32[15,2,32,128]{3,2,1,0:T(8,128)} copy(f32[15,2,32,128]{3,2,1,0:T(8,128)S(1)} %bitcast.7) | data formatting | bytes 983040
  58.8 0.8 %copy.10 = f32[15,2,32,128]{3,2,1,0:T(8,128)} copy(f32[15,2,32,128]{3,2,1,0:T(8,128)S(1)} %bitcast.6) | data formatting | bytes 983040
Async XLA Ops:
  0.6 1.0 %copy-start = (f32[15,2,32,128]{3,2,1,0:T(8,128)S(1)}, f32[15,2,32,128]{3,2,1,0:T(8,128)}, u32[]{:S(2)}) copy-start(f32[15,2,32,128]{3,2,1,0:T(8,128)} %param.5) | copy-start | bytes 1474564
  1.7 1.0 %copy-start.1 = (f32[15,2,32,128]{3,2,1,0:T(8,128)S(1)}, f32[15,2,32,128]{3,2,1,0:T(8,128)}, u32[]{:S(2)}) copy-start(f32[15,2,32,128]{3,2,1,0:T(8,128)} %param.6) | copy-start | bytes 1474564
  2.7 0.9 %copy-start.2 = (f32[8,2,32,128]{3,2,1,0:T(8,128)S(1)}, f32[8,2,32,128]{3,2,1,0:T(8,128)}, u32[]{:S(2)}) copy-start(f32[8,2,32,128]{3,2,1,0:T(8,128)} %a_hbm.1) | copy-start | bytes 786436
  3.6 0.8 %copy-start.3 = (s32[3,2880]{1,0:T(4,128)S(1)}, s32[3,2880]{1,0:T(4,128)}, u32[]{:S(2)}) copy-start(s32[3,2880]{1,0:T(4,128)} %tri_hbm.1) | copy-start | bytes 103684
  4.4 0.7 %copy-start.4 = (f32[2880]{0:T(1024)S(1)}, f32[2880]{0:T(1024)}, u32[]{:S(2)}) copy-start(f32[2880]{0:T(1024)} %cf_hbm.1) | copy-start | bytes 34564

commit v2 on v1

--- a/solution.py
+++ b/solution.py
@@ -16,6 +16,7 @@
 LANES = 128
 OWN = ROWS // GROUPS
 ENTRIES = 2880
+LAG = 4
 WIDE = GROUPS * PAD
 relax_weight = 0.8
 
@@ -67,8 +68,8 @@
 ):
     m = lax.axis_index("modes")
     s = lax.axis_index("space")
-    s_up = lax.rem(s + 1, space_count)
-    s_dn = lax.rem(s + space_count - 1, space_count)
+    has_dn = s > 0
+    has_up = s < space_count - 1
 
     def peer_to(d):
         return lax.rem(m + d, GROUPS)
@@ -82,8 +83,14 @@
     barrier = pltpu.get_barrier_semaphore()
     for d in range(1, GROUPS):
         pl.semaphore_signal(barrier, inc=1, device_id=(peer_to(d), s), device_id_type=MESH)
-    for side in (s_up, s_dn):
-        pl.semaphore_signal(barrier, inc=1, device_id=(m, side), device_id_type=MESH)
+
+    @pl.when(has_dn)
+    def _():
+        pl.semaphore_signal(barrier, inc=1, device_id=(m, s - 1), device_id_type=MESH)
+
+    @pl.when(has_up)
+    def _():
+        pl.semaphore_signal(barrier, inc=1, device_id=(m, s + 1), device_id_type=MESH)
 
     load_p = pltpu.make_async_copy(p_hbm, p_v.at[0 : LOCAL * 64], in_sem.at[0])
     load_a = pltpu.make_async_copy(a_hbm, a_v.at[:, 1:3], in_sem.at[1])
@@ -96,7 +103,6 @@
     p_v[LOCAL * 64 :, :] = jnp.zeros((64, LANES), F32)
     t[:, 0] = jnp.zeros((LAYERS, PAD, LANES), F32)
     t[:, ROWS + 1] = jnp.zeros((LAYERS, PAD, LANES), F32)
-    r_out[...] = jnp.zeros(r_out.shape, F32)
     load_p.wait()
 
     def stage(row, carry):
@@ -128,7 +134,7 @@
             dst_ref=q.at[0 if up else 3, 1 : OWN + 1, rows, :],
             send_sem=sems[0].at[d],
             recv_sem=sems[1].at[d],
-            device_id=(m, s_up if up else s_dn),
+            device_id=(m, s + 1 if up else s - 1),
             device_id_type=MESH,
         )
 
@@ -138,29 +144,56 @@
             dst_ref=a_v.at[:, 0 if up else 3],
             send_sem=perm_send.at[1 if up else 0],
             recv_sem=perm_recv.at[1 if up else 0],
-            device_id=(m, s_up if up else s_dn),
+            device_id=(m, s + 1 if up else s - 1),
             device_id_type=MESH,
         )
 
-    def send_back(d):
+    def send_back(d, layer):
         g = peer_to(d)
         return pltpu.make_async_remote_copy(
-            src_ref=r_out.at[g],
-            dst_ref=ret.at[:, pl.ds(pl.multiple_of(m * OWN * PAD, OWN * PAD), OWN * PAD), :],
-            send_sem=ret_send.at[d],
-            recv_sem=ret_recv.at[d],
+            src_ref=r_out.at[g, layer],
+            dst_ref=ret.at[layer, pl.ds(pl.multiple_of(m * OWN * PAD, OWN * PAD), OWN * PAD), :],
+            send_sem=ret_send.at[d, layer],
+            recv_sem=ret_recv.at[d, layer],
             device_id=(g, s),
             device_id_type=MESH,
         )
 
-    pl.semaphore_wait(barrier, GROUPS - 1 + 2)
+    def both_ways(make, act):
+        @pl.when(has_up)
+        def _():
+            getattr(make(True), act)()
+
+        @pl.when(has_dn)
+        def _():
+            getattr(make(False), act)()
+
+    def arrived(make):
+        @pl.when(has_dn)
+        def _():
+            make(True).wait_recv()
+
+        @pl.when(has_up)
+        def _():
+            make(False).wait_recv()
+
+    neighbours = GROUPS - 1 + has_dn.astype(jnp.int32) + has_up.astype(jnp.int32)
+    pl.semaphore_wait(barrier, neighbours)
     for d in range(1, GROUPS):
         send_block(d).start()
     load_a.wait()
-    perm_halo(True).start()
-    perm_halo(False).start()
-    halo(0, True).start()
-    halo(0, False).start()
+    both_ways(perm_halo, "start")
+    both_ways(functools.partial(halo, 0), "start")
+
+    @pl.when(jnp.logical_not(has_dn))
+    def _():
+        q[0] = jnp.zeros(q.shape[1:], F32)
+        a_v[:, 0] = jnp.zeros((KA, ROWS, LANES), F32)
+
+    @pl.when(jnp.logical_not(has_up))
+    def _():
+        q[3] = jnp.zeros(q.shape[1:], F32)
+        a_v[:, 3] = jnp.zeros((KA, ROWS, LANES), F32)
 
     load_t.wait()
     load_c.wait()
@@ -188,16 +221,14 @@
             hi = one.astype(BF16)
             lo = (one - hi.astype(F32)).astype(BF16)
             for side in range(2):
-                w_mat[2 * c + part, 0:WIDE, side * WIDE : (side + 1) * WIDE] = hi
-                w_mat[2 * c + part, WIDE:, side * WIDE : (side + 1) * WIDE] = lo
+                at = pl.multiple_of(c * 4 * WIDE + (2 * part + side) * WIDE, WIDE)
+                w_mat[0:WIDE, pl.ds(at, WIDE)] = hi
+                w_mat[WIDE:, pl.ds(at, WIDE)] = lo
         return carry
 
     lax.fori_loop(0, GROUPS // 2, table, 0)
 
-    perm_halo(True).wait_recv()
-    perm_halo(False).wait_recv()
-    has_dn = (s > 0).astype(F32)
-    has_up = (s < space_count - 1).astype(F32)
+    arrived(perm_halo)
     row_ids = lax.broadcasted_iota(jnp.int32, (ROWS, LANES), 0)
     lane_ids = lax.broadcasted_iota(jnp.int32, (ROWS, LANES), 1)
 
@@ -206,10 +237,6 @@
             a = a_v[k, layer + 1]
             low = a_v[k, layer]
             high = a_v[k, layer + 2]
-            if layer == 0:
-                low = low * has_dn
-            else:
-                high = high * has_up
             sides = (
                 low,
                 high,
@@ -235,15 +262,9 @@
         for layer in range(LAYERS):
             for r in range(OWN):
                 p = q[layer + 1, r + 1, rows, :]
-                low = q[layer, r + 1, rows, :]
-                high = q[layer + 2, r + 1, rows, :]
-                if layer == 0:
-                    low = low * has_dn
-                else:
-                    high = high * has_up
                 diffs = (
-                    p - low,
-                    p - high,
+                    p - q[layer, r + 1, rows, :],
+                    p - q[layer + 2, r + 1, rows, :],
                     p - q[layer + 1, r, rows, :],
                     p - q[layer + 1, r + 2, rows, :],
                     p - jnp.where(lanes > 0, pltpu.roll(p, 1, 1), 0.0),
@@ -257,41 +278,45 @@
                         total = term if total is None else total + term
                     hi = total.astype(BF16)
                     lo = (total - hi.astype(F32)).astype(BF16)
-                    m_buf[k * PAD : (k + 1) * PAD, at : at + LANES] = hi
-                    m_buf[WIDE + k * PAD : WIDE + (k + 1) * PAD, at : at + LANES] = lo
-            for n in range(OWN // 2):
-                at = (layer * OWN + 2 * n) * LANES
-                prod = jnp.dot(
-                    w_mat[g], m_buf[:, at : at + 2 * LANES], preferred_element_type=F32
-                )
-                prod = prod[:WIDE] + prod[WIDE:]
-                for part in range(2):
-                    r = 2 * n + part
-                    for go in range(GROUPS):
-                        r_out[go, layer, r * PAD : (r + 1) * PAD, :] += prod[
-                            go * PAD : (go + 1) * PAD, part * LANES : (part + 1) * LANES
-                        ]
+                    for part, piece in enumerate((hi, lo)):
+                        to = pl.multiple_of((2 * g + part) * WIDE + k * PAD, PAD)
+                        m_buf[pl.ds(to, PAD), at : at + LANES] = piece
 
     def step(d, carry):
         @pl.when(d < GROUPS)
         def _():
             send_block(d).wait_recv()
-            halo(d, True).start()
-            halo(d, False).start()
-
-        halo(d - 1, True).wait_recv()
-        halo(d - 1, False).wait_recv()
-        chunk(d - 1)
-        return carry
-
-    lax.fori_loop(1, GROUPS + 1, step, 0)
-
-    for d in range(1, GROUPS):
-        send_back(d).start()
+            both_ways(functools.partial(halo, d), "start")
+
+        @pl.when(d >= LAG)
+        def _():
+            arrived(functools.partial(halo, d - LAG))
+            chunk(d - LAG)
+
+        return carry
+
+    lax.fori_loop(1, GROUPS + LAG, step, 0)
+
+    for layer in range(LAYERS):
+        half = OWN * LANES
+        prod = jnp.dot(
+            w_mat[...],
+            m_buf[:, layer * half : (layer + 1) * half],
+            preferred_element_type=F32,
+        )
+        prod = prod[:WIDE] + prod[WIDE:]
+        for r in range(OWN):
+            for go in range(GROUPS):
+                r_out[go, layer, r * PAD : (r + 1) * PAD, :] = prod[
+                    go * PAD : (go + 1) * PAD, r * LANES : (r + 1) * LANES
+                ]
+        for d in range(1, GROUPS):
+            send_back(d, layer).start()
     ret[:, pl.ds(pl.multiple_of(m * OWN * PAD, OWN * PAD), OWN * PAD), :] = r_out[m]
 
-    own_rows = w_mat[m, mode_rows(m), 0:WIDE].astype(F32) + w_mat[
-        m, pl.ds(pl.multiple_of(WIDE + m * PAD, PAD), PAD), 0:WIDE
+    own_cols = pl.ds(pl.multiple_of(2 * WIDE * m, 2 * WIDE), WIDE)
+    own_rows = w_mat[mode_rows(m), own_cols].astype(F32) + w_mat[
+        pl.ds(pl.multiple_of(WIDE + m * PAD, PAD), PAD), own_cols
     ].astype(F32)
     sub = lax.broadcasted_iota(jnp.int32, (PAD, LANES), 0)
     lane = lax.broadcasted_iota(jnp.int32, (PAD, LANES), 1)
@@ -314,19 +339,18 @@
 
     lax.fori_loop(0, LOCAL, scales, 0)
 
-    for d in range(1, GROUPS):
-        send_back(d).wait_recv()
-
-    def finish(j, carry):
-        for layer in range(LAYERS):
-            for r8 in range(ROWS // 8):
-                got = ret[layer, pl.ds(r8 * 8 * PAD + j, 8, stride=PAD), :]
-                at = pl.ds(pl.multiple_of(j * 64 + layer * ROWS + r8 * 8, 8), 8)
-                oa_v[at, :] = got
-                or_v[at, :] = base_v[at, :] - got * inv_v[at, :]
-        return carry
-
-    lax.fori_loop(0, LOCAL, finish, 0)
+    def finish(layer, j, carry):
+        for r8 in range(ROWS // 8):
+            got = ret[layer, pl.ds(r8 * 8 * PAD + j, 8, stride=PAD), :]
+            at = pl.ds(pl.multiple_of(j * 64 + layer * ROWS + r8 * 8, 8), 8)
+            oa_v[at, :] = got
+            or_v[at, :] = base_v[at, :] - got * inv_v[at, :]
+        return carry
+
+    for layer in range(LAYERS):
+        for d in range(1, GROUPS):
+            send_back(d, layer).wait_recv()
+        lax.fori_loop(0, LOCAL, functools.partial(finish, layer), 0)
     out_a = pltpu.make_async_copy(oa_v, out_a_hbm, out_sem.at[0])
     out_r = pltpu.make_async_copy(or_v, out_r_hbm, out_sem.at[1])
     out_a.start()
@@ -334,12 +358,11 @@
 
     for d in range(1, GROUPS):
         send_block(d).wait_send()
-        send_back(d).wait_send()
+        for layer in range(LAYERS):
+            send_back(d, layer).wait_send()
     for d in range(GROUPS):
-        halo(d, True).wait_send()
-        halo(d, False).wait_send()
-    perm_halo(True).wait_send()
-    perm_halo(False).wait_send()
+        both_ways(functools.partial(halo, d), "wait_send")
+    both_ways(perm_halo, "wait_send")
     out_a.wait()
     out_r.wait()
 
@@ -352,7 +375,7 @@
         applied, relaxed = pl.pallas_call(
             functools.partial(kernel, space_count),
             out_shape=[jax.ShapeDtypeStruct(cells, F32)] * 2,
-            in_specs=[pl.BlockSpec(memory_space=pl.ANY)] * 5,
+            in_specs=[pl.BlockSpec(memory_space=pltpu.HBM)] * 5,
             out_specs=[pl.BlockSpec(memory_space=pl.ANY)] * 2,
             scratch_shapes=[
                 pltpu.VMEM((PAD * LAYERS * ROWS, LANES), F32),
@@ -364,9 +387,9 @@
                 pltpu.VMEM((LAYERS + 2, OWN + 2, WIDE, LANES), F32),
                 pltpu.VMEM((GROUPS, LAYERS, OWN * PAD, LANES), F32),
                 pltpu.VMEM((LAYERS, ROWS * PAD, LANES), F32),
-                pltpu.VMEM((GROUPS, 2 * WIDE, 2 * WIDE), BF16),
+                pltpu.VMEM((2 * WIDE, GROUPS * 2 * WIDE), BF16),
                 pltpu.VMEM((2 * WIDE, ENTRIES), BF16),
-                pltpu.VMEM((2 * WIDE, LAYERS * OWN * LANES), BF16),
+                pltpu.VMEM((GROUPS * 2 * WIDE, LAYERS * OWN * LANES), BF16),
                 pltpu.VMEM((6, KA, LAYERS, ROWS, LANES), F32),
                 pltpu.VMEM((KA, LAYERS, ROWS, LANES), F32),
                 pltpu.VMEM((KA, PAD, LANES), F32),
@@ -379,9 +402,9 @@
             ]
             + [pltpu.SemaphoreType.DMA((GROUPS,))] * 6
             + [pltpu.SemaphoreType.DMA((2,))] * 2
-            + [pltpu.SemaphoreType.DMA((GROUPS,))] * 2,
+            + [pltpu.SemaphoreType.DMA((GROUPS, LAYERS))] * 2,
             compiler_params=pltpu.CompilerParams(
-                collective_id=0, has_side_effects=True, vmem_limit_bytes=48 * 1024 * 1024
+                collective_id=0, has_side_effects=True, vmem_limit_bytes=60 * 1024 * 1024
             ),
         )(
             pressure.reshape(cells),

time: 59.9 us -> 43.3 us (0.72)
  the two profiles are of different devices: /device:TPU:56 before, /device:TPU:7 now
where the time goes in v2:
time: 43.3 us; the launch traced here: 43.1 us
  Pallas kernels  39.8 us (92%)
  local copies, waits for them, and re-layouts  2.69 us (6%)
  between operations  0.65 us (2%)
    pallas_call x1, Pallas kernels, on_device(): pl.pallas_call(functools.partial(kernel, space_count), out_shape=[jax.Sha...  39.8 us
    unnamed x4, local copies, waits for them, and re-layouts  2.69 us

profile of v2, /device:TPU:7, one launch (start us, length us, event | category | flops | bytes accessed | tf_op | source)
XLA Modules:
  0.0 43.1 jit_solution(17976731498319725604)
XLA Ops:
  0.6 39.8 %shard_map.68 = (f32[960,128]{1,0:T(8,128)}, f32[960,128]{1,0:T(8,128)}) custom-call(f32[960,128]{1,0:T(8,128)} %bitcast.4, f32[960,128]{1,0:T(8,128)} %bitcast.5, f32[8,2,32,128]{3,2,1,0:T(8,128)} %a_hbm.1, s32[3,2880]{1,0:T(4,128)} %tri_hbm.1, f32[2880]{0:T(1024)} %cf_hbm.1), custom_call_target="tpu_custom_call" | custom-call | tf_op jit(solution)/shard_map/pallas_call | solution.py:375
  40.4 0.0 copy-start
  40.4 1.9 %copy.9 = f32[15,2,32,128]{3,2,1,0:T(8,128)} copy(f32[15,2,32,128]{3,2,1,0:T(8,128)} %bitcast.7) | data formatting | bytes 983040
  42.4 0.0 copy-done
  42.4 0.8 %copy.10 = f32[15,2,32,128]{3,2,1,0:T(8,128)} copy(f32[15,2,32,128]{3,2,1,0:T(8,128)S(1)} %bitcast.6) | data formatting | bytes 983040
Async XLA Ops:
  40.4 1.9 %copy-start = (f32[960,128]{1,0:T(8,128)S(1)}, f32[960,128]{1,0:T(8,128)}, u32[]{:S(2)}) copy-start(f32[960,128]{1,0:T(8,128)} %get-tuple-element.5) | copy-start | bytes 1474564

commit v3 on v2

--- a/solution.py
+++ b/solution.py
@@ -17,6 +17,8 @@
 OWN = ROWS // GROUPS
 ENTRIES = 2880
 LAG = 4
+EDGE = 8
+DATA = slice(EDGE, EDGE + ROWS)
 WIDE = GROUPS * PAD
 relax_weight = 0.8
 
@@ -33,7 +35,8 @@
     tri_hbm,
     cf_hbm,
     out_a_hbm,
-    out_r_hbm,
+    out_b_hbm,
+    out_i_hbm,
     p_v,
     s_v,
     a_v,
@@ -47,12 +50,13 @@
     a_hot,
     m_buf,
     w_f,
+    a_str,
+    a_y,
     dg,
     cdb,
     inv_v,
     base_v,
     oa_v,
-    or_v,
     in_sem,
     out_sem,
     a2a_send,
@@ -63,6 +67,8 @@
     high_recv,
     perm_send,
     perm_recv,
+    str_send,
+    str_recv,
     ret_send,
     ret_recv,
 ):
@@ -93,7 +99,7 @@
         pl.semaphore_signal(barrier, inc=1, device_id=(m, s + 1), device_id_type=MESH)
 
     load_p = pltpu.make_async_copy(p_hbm, p_v.at[0 : LOCAL * 64], in_sem.at[0])
-    load_a = pltpu.make_async_copy(a_hbm, a_v.at[:, 1:3], in_sem.at[1])
+    load_a = pltpu.make_async_copy(a_hbm, a_v.at[:, 1:3, DATA], in_sem.at[1])
     load_t = pltpu.make_async_copy(tri_hbm, tri_v, in_sem.at[2])
     load_c = pltpu.make_async_copy(cf_hbm, cf_v, in_sem.at[3])
     load_s = pltpu.make_async_copy(s_hbm, s_v, in_sem.at[4])
@@ -140,10 +146,20 @@
 
     def perm_halo(up):
         return pltpu.make_async_remote_copy(
-            src_ref=a_v.at[:, 2 if up else 1],
-            dst_ref=a_v.at[:, 0 if up else 3],
+            src_ref=a_v.at[:, 2 if up else 1, DATA],
+            dst_ref=a_v.at[:, 0 if up else 3, DATA],
             send_sem=perm_send.at[1 if up else 0],
             recv_sem=perm_recv.at[1 if up else 0],
+            device_id=(m, s + 1 if up else s - 1),
+            device_id_type=MESH,
+        )
+
+    def strip(up):
+        return pltpu.make_async_remote_copy(
+            src_ref=a_str.at[2 if up else 1],
+            dst_ref=a_str.at[0 if up else 3],
+            send_sem=str_send.at[1 if up else 0],
+            recv_sem=str_recv.at[1 if up else 0],
             device_id=(m, s + 1 if up else s - 1),
             device_id_type=MESH,
         )
@@ -177,23 +193,34 @@
         def _():
             make(False).wait_recv()
 
+    load_a.wait()
+    for layer in range(LAYERS):
+        a_v[:, layer + 1, 0:EDGE] = jnp.zeros((KA, EDGE, LANES), F32)
+        a_v[:, layer + 1, EDGE + ROWS :] = jnp.zeros((KA, EDGE, LANES), F32)
+        for k in range(KA):
+            to = slice(k * OWN, (k + 1) * OWN)
+            a_str[layer + 1, to, :] = a_v[k, layer + 1, pl.ds(EDGE + m * OWN, OWN), :]
+            a_y[0, layer, to, :] = a_v[k, layer + 1, pl.ds(EDGE + m * OWN - 1, OWN), :]
+            a_y[1, layer, to, :] = a_v[k, layer + 1, pl.ds(EDGE + m * OWN + 1, OWN), :]
+
     neighbours = GROUPS - 1 + has_dn.astype(jnp.int32) + has_up.astype(jnp.int32)
     pl.semaphore_wait(barrier, neighbours)
+    both_ways(strip, "start")
     for d in range(1, GROUPS):
         send_block(d).start()
-    load_a.wait()
-    both_ways(perm_halo, "start")
     both_ways(functools.partial(halo, 0), "start")
 
     @pl.when(jnp.logical_not(has_dn))
     def _():
         q[0] = jnp.zeros(q.shape[1:], F32)
-        a_v[:, 0] = jnp.zeros((KA, ROWS, LANES), F32)
+        a_v[:, 0, DATA] = jnp.zeros((KA, ROWS, LANES), F32)
+        a_str[0] = jnp.zeros((KA * OWN, LANES), F32)
 
     @pl.when(jnp.logical_not(has_up))
     def _():
         q[3] = jnp.zeros(q.shape[1:], F32)
-        a_v[:, 3] = jnp.zeros((KA, ROWS, LANES), F32)
+        a_v[:, 3, DATA] = jnp.zeros((KA, ROWS, LANES), F32)
+        a_str[3] = jnp.zeros((KA * OWN, LANES), F32)
 
     load_t.wait()
     load_c.wait()
@@ -228,32 +255,20 @@
 
     lax.fori_loop(0, GROUPS // 2, table, 0)
 
-    arrived(perm_halo)
-    row_ids = lax.broadcasted_iota(jnp.int32, (ROWS, LANES), 0)
+    arrived(strip)
     lane_ids = lax.broadcasted_iota(jnp.int32, (ROWS, LANES), 1)
 
-    def weights(k, carry):
-        for layer in range(LAYERS):
-            a = a_v[k, layer + 1]
-            low = a_v[k, layer]
-            high = a_v[k, layer + 2]
-            sides = (
-                low,
-                high,
-                jnp.where(row_ids > 0, pltpu.roll(a, 1, 0), 0.0),
-                jnp.where(row_ids < ROWS - 1, pltpu.roll(a, ROWS - 1, 0), 0.0),
-                jnp.where(lane_ids > 0, pltpu.roll(a, 1, 1), 0.0),
-                jnp.where(lane_ids < LANES - 1, pltpu.roll(a, LANES - 1, 1), 0.0),
-            )
-            total = jnp.zeros((ROWS, LANES), F32)
-            for f, side in enumerate(sides):
-                w = 0.5 * (a + side)
-                w_f[f, k, layer] = w
-                total = total + w
-            dg[k, layer] = total
-        return carry
-
-    lax.fori_loop(0, KA, weights, 0)
+    def beside(a):
+        return (
+            jnp.where(lane_ids > 0, pltpu.roll(a, 1, 1), 0.0),
+            jnp.where(lane_ids < LANES - 1, pltpu.roll(a, LANES - 1, 1), 0.0),
+        )
+
+    for layer in range(LAYERS):
+        a = a_str[layer + 1]
+        sides = (a_str[layer], a_str[layer + 2], a_y[0, layer], a_y[1, layer]) + beside(a)
+        for f, side in enumerate(sides):
+            w_f[f, layer] = a + side
 
     def chunk(d):
         g = peer_from(d)
@@ -274,7 +289,7 @@
                 for k in range(KA):
                     total = None
                     for f in range(6):
-                        term = w_f[f, k, layer, pl.ds(m * OWN + r, 1), :] * diffs[f]
+                        term = w_f[f, layer, k * OWN + r : k * OWN + r + 1, :] * diffs[f]
                         total = term if total is None else total + term
                     hi = total.astype(BF16)
                     lo = (total - hi.astype(F32)).astype(BF16)
@@ -287,6 +302,10 @@
         def _():
             send_block(d).wait_recv()
             both_ways(functools.partial(halo, d), "start")
+
+        @pl.when(d == GROUPS)
+        def _():
+            both_ways(perm_halo, "start")
 
         @pl.when(d >= LAG)
         def _():
@@ -324,6 +343,24 @@
         picked = jnp.where(lane == sub + k * PAD, own_rows, 0.0)
         cdb[k] = jnp.broadcast_to(jnp.sum(picked, axis=1, keepdims=True), (PAD, LANES))
 
+    arrived(perm_halo)
+
+    def diagonal(k, carry):
+        for layer in range(LAYERS):
+            a = a_v[k, layer + 1, DATA]
+            sides = (
+                a_v[k, layer, DATA],
+                a_v[k, layer + 2, DATA],
+                a_v[k, layer + 1, EDGE - 1 : EDGE - 1 + ROWS],
+                a_v[k, layer + 1, EDGE + 1 : EDGE + 1 + ROWS],
+            ) + beside(a)
+            total = 6.0 * a
+            for side in sides:
+                total = total + side
+            dg[k, layer] = 0.5 * total
+        return carry
+
+    lax.fori_loop(0, KA, diagonal, 0)
     load_s.wait()
 
     def scales(j, carry):
@@ -344,17 +381,19 @@
             got = ret[layer, pl.ds(r8 * 8 * PAD + j, 8, stride=PAD), :]
             at = pl.ds(pl.multiple_of(j * 64 + layer * ROWS + r8 * 8, 8), 8)
             oa_v[at, :] = got
-            or_v[at, :] = base_v[at, :] - got * inv_v[at, :]
-        return carry
+        return carry
+
+    out_b = pltpu.make_async_copy(base_v, out_b_hbm, out_sem.at[0])
+    out_i = pltpu.make_async_copy(inv_v, out_i_hbm, out_sem.at[1])
+    out_b.start()
+    out_i.start()
 
     for layer in range(LAYERS):
         for d in range(1, GROUPS):
             send_back(d, layer).wait_recv()
         lax.fori_loop(0, LOCAL, functools.partial(finish, layer), 0)
-    out_a = pltpu.make_async_copy(oa_v, out_a_hbm, out_sem.at[0])
-    out_r = pltpu.make_async_copy(or_v, out_r_hbm, out_sem.at[1])
+    out_a = pltpu.make_async_copy(oa_v, out_a_hbm, out_sem.at[2])
     out_a.start()
-    out_r.start()
 
     for d in range(1, GROUPS):
         send_block(d).wait_send()
@@ -363,8 +402,10 @@
     for d in range(GROUPS):
         both_ways(functools.partial(halo, d), "wait_send")
     both_ways(perm_halo, "wait_send")
+    both_ways(strip, "wait_send")
+    out_b.wait()
+    out_i.wait()
     out_a.wait()
-    out_r.wait()
 
 
 def solution(mesh):
@@ -372,15 +413,15 @@
     cells = (LOCAL * LAYERS * ROWS, LANES)
 
     def on_device(pressure, source, perm_modes, triples, coeffs):
-        applied, relaxed = pl.pallas_call(
+        doubled, base, inv = pl.pallas_call(
             functools.partial(kernel, space_count),
-            out_shape=[jax.ShapeDtypeStruct(cells, F32)] * 2,
+            out_shape=[jax.ShapeDtypeStruct(cells, F32)] * 3,
             in_specs=[pl.BlockSpec(memory_space=pltpu.HBM)] * 5,
-            out_specs=[pl.BlockSpec(memory_space=pl.ANY)] * 2,
+            out_specs=[pl.BlockSpec(memory_space=pl.ANY)] * 3,
             scratch_shapes=[
                 pltpu.VMEM((PAD * LAYERS * ROWS, LANES), F32),
                 pltpu.VMEM(cells, F32),
-                pltpu.VMEM((KA, LAYERS + 2, ROWS, LANES), F32),
+                pltpu.VMEM((KA, LAYERS + 2, ROWS + 2 * EDGE, LANES), F32),
                 pltpu.VMEM((3, ENTRIES), jnp.int32),
                 pltpu.VMEM((ENTRIES,), F32),
                 pltpu.VMEM((LAYERS, ROWS + 2, PAD, LANES), F32),
@@ -390,18 +431,19 @@
                 pltpu.VMEM((2 * WIDE, GROUPS * 2 * WIDE), BF16),
                 pltpu.VMEM((2 * WIDE, ENTRIES), BF16),
                 pltpu.VMEM((GROUPS * 2 * WIDE, LAYERS * OWN * LANES), BF16),
-                pltpu.VMEM((6, KA, LAYERS, ROWS, LANES), F32),
+                pltpu.VMEM((6, LAYERS, KA * OWN, LANES), F32),
+                pltpu.VMEM((LAYERS + 2, KA * OWN, LANES), F32),
+                pltpu.VMEM((2, LAYERS, KA * OWN, LANES), F32),
                 pltpu.VMEM((KA, LAYERS, ROWS, LANES), F32),
                 pltpu.VMEM((KA, PAD, LANES), F32),
                 pltpu.VMEM(cells, F32),
                 pltpu.VMEM(cells, F32),
                 pltpu.VMEM(cells, F32),
-                pltpu.VMEM(cells, F32),
                 pltpu.SemaphoreType.DMA((5,)),
-                pltpu.SemaphoreType.DMA((2,)),
+                pltpu.SemaphoreType.DMA((3,)),
             ]
             + [pltpu.SemaphoreType.DMA((GROUPS,))] * 6
-            + [pltpu.SemaphoreType.DMA((2,))] * 2
+            + [pltpu.SemaphoreType.DMA((2,))] * 4
             + [pltpu.SemaphoreType.DMA((GROUPS, LAYERS))] * 2,
             compiler_params=pltpu.CompilerParams(
                 collective_id=0, has_side_effects=True, vmem_limit_bytes=60 * 1024 * 1024
@@ -413,6 +455,8 @@
             triples,
             coeffs,
         )
+        applied = 0.5 * doubled
+        relaxed = base - applied * inv
         return applied.reshape(pressure.shape), relaxed.reshape(pressure.shape)
 
     return jax.shard_map(

time: 43.3 us -> 39.8 us (0.919)
  the two profiles are of different devices: /device:TPU:7 before, /device:TPU:71 now
where the time goes in v3:
time: 39.8 us; the launch traced here: 39.7 us
  Pallas kernels  36.7 us (92%)
  other arithmetic  2.35 us (6%)
  between operations  0.64 us (2%)
    pallas_call x1, Pallas kernels, on_device(): pl.pallas_call(functools.partial(kernel, space_count), out_shape=[jax.Sha...  36.7 us
    sub x1, other arithmetic, on_device(): relaxed = base - applied * inv  2.35 us

profile of v3, /device:TPU:71, one launch (start us, length us, event | category | flops | bytes accessed | tf_op | source)
XLA Modules:
  0.0 39.7 jit_solution(9929709467384316068)
XLA Ops:
  0.6 36.7 %shard_map.68 = (f32[960,128]{1,0:T(8,128)}, f32[960,128]{1,0:T(8,128)}, f32[960,128]{1,0:T(8,128)}) custom-call(f32[960,128]{1,0:T(8,128)} %bitcast.6, f32[960,128]{1,0:T(8,128)} %bitcast.7, f32[8,2,32,128]{3,2,1,0:T(8,128)} %a_hbm.1, s32[3,2880]{1,0:T(4,128)} %tri_hbm.1, f32[2880]{0:T(1024)} %cf_hbm.1), custom_call_target="tpu_custom_call" | custom-call | tf_op jit(solution)/shard_map/pallas_call | solution.py:416
  37.3 2.3 %multiply_subtract_fusion = (f32[960,128]{1,0:T(8,128)}, f32[960,128]{1,0:T(8,128)}) fusion(f32[960,128]{1,0:T(8,128)} %get-tuple-element.6, f32[960,128]{1,0:T(8,128)} %get-tuple-element.7, f32[960,128]{1,0:T(8,128)} %get-tuple-element.5), kind=kLoop, calls=%fused_computation | loop fusion | flops 368640 | bytes 2457600 | tf_op jit(solution)/shard_map/sub | solution.py:459

commit v4 on v3

--- a/solution.py
+++ b/solution.py
@@ -17,6 +17,10 @@
 OWN = ROWS // GROUPS
 ENTRIES = 2880
 LAG = 4
+WAVES = 2
+STEP = OWN // WAVES
+COMES = ((0, 4), (4, 6))
+HANDED = ((1, 4), (4, 5))
 EDGE = 8
 DATA = slice(EDGE, EDGE + ROWS)
 WIDE = GROUPS * PAD
@@ -121,25 +125,27 @@
     lax.fori_loop(0, ROWS, stage, 0)
     q[1:3, :, mode_rows(m), :] = t[:, pl.ds(m * OWN, OWN + 2), :, :]
 
-    def send_block(d):
+    def send_block(wave, d):
         g = peer_to(d)
+        first, last = COMES[wave]
         return pltpu.make_async_remote_copy(
-            src_ref=t.at[:, pl.ds(g * OWN, OWN + 2)],
-            dst_ref=q.at[1:3, :, mode_rows(m), :],
-            send_sem=a2a_send.at[d],
-            recv_sem=a2a_recv.at[d],
+            src_ref=t.at[:, pl.ds(g * OWN + first, last - first)],
+            dst_ref=q.at[1:3, first:last, mode_rows(m), :],
+            send_sem=a2a_send.at[wave, d],
+            recv_sem=a2a_recv.at[wave, d],
             device_id=(g, s),
             device_id_type=MESH,
         )
 
-    def halo(d, up):
+    def halo(wave, d, up):
         rows = mode_rows(peer_from(d))
+        first, last = HANDED[wave]
         sems = (high_send, high_recv) if up else (low_send, low_recv)
         return pltpu.make_async_remote_copy(
-            src_ref=q.at[2 if up else 1, 1 : OWN + 1, rows, :],
-            dst_ref=q.at[0 if up else 3, 1 : OWN + 1, rows, :],
-            send_sem=sems[0].at[d],
-            recv_sem=sems[1].at[d],
+            src_ref=q.at[2 if up else 1, first:last, rows, :],
+            dst_ref=q.at[0 if up else 3, first:last, rows, :],
+            send_sem=sems[0].at[wave, d],
+            recv_sem=sems[1].at[wave, d],
             device_id=(m, s + 1 if up else s - 1),
             device_id_type=MESH,
         )
@@ -164,13 +170,16 @@
             device_id_type=MESH,
         )
 
-    def send_back(d, layer):
+    def ret_rows(wave):
+        return pl.ds(pl.multiple_of((m * OWN + wave * STEP) * PAD, STEP * PAD), STEP * PAD)
+
+    def send_back(wave, d):
         g = peer_to(d)
         return pltpu.make_async_remote_copy(
-            src_ref=r_out.at[g, layer],
-            dst_ref=ret.at[layer, pl.ds(pl.multiple_of(m * OWN * PAD, OWN * PAD), OWN * PAD), :],
-            send_sem=ret_send.at[d, layer],
-            recv_sem=ret_recv.at[d, layer],
+            src_ref=r_out.at[g, wave],
+            dst_ref=ret.at[:, ret_rows(wave), :],
+            send_sem=ret_send.at[wave, d],
+            recv_sem=ret_recv.at[wave, d],
             device_id=(g, s),
             device_id_type=MESH,
         )
@@ -206,9 +215,11 @@
     neighbours = GROUPS - 1 + has_dn.astype(jnp.int32) + has_up.astype(jnp.int32)
     pl.semaphore_wait(barrier, neighbours)
     both_ways(strip, "start")
-    for d in range(1, GROUPS):
-        send_block(d).start()
-    both_ways(functools.partial(halo, 0), "start")
+    for wave in range(WAVES):
+        for d in range(1, GROUPS):
+            send_block(wave, d).start()
+    for wave in range(WAVES):
+        both_ways(functools.partial(halo, wave, 0), "start")
 
     @pl.when(jnp.logical_not(has_dn))
     def _():
@@ -270,12 +281,12 @@
         for f, side in enumerate(sides):
             w_f[f, layer] = a + side
 
-    def chunk(d):
+    def chunk(wave, d):
         g = peer_from(d)
         rows = mode_rows(g)
         lanes = lax.broadcasted_iota(jnp.int32, (PAD, LANES), 1)
         for layer in range(LAYERS):
-            for r in range(OWN):
+            for r in range(wave * STEP, (wave + 1) * STEP):
                 p = q[layer + 1, r + 1, rows, :]
                 diffs = (
                     p - q[layer, r + 1, rows, :],
@@ -285,7 +296,7 @@
                     p - jnp.where(lanes > 0, pltpu.roll(p, 1, 1), 0.0),
                     p - jnp.where(lanes < LANES - 1, pltpu.roll(p, LANES - 1, 1), 0.0),
                 )
-                at = (layer * OWN + r) * LANES
+                at = (wave * LAYERS * STEP + layer * STEP + r - wave * STEP) * LANES
                 for k in range(KA):
                     total = None
                     for f in range(6):
@@ -297,41 +308,40 @@
                         to = pl.multiple_of((2 * g + part) * WIDE + k * PAD, PAD)
                         m_buf[pl.ds(to, PAD), at : at + LANES] = piece
 
-    def step(d, carry):
+    def step(wave, d, carry):
         @pl.when(d < GROUPS)
         def _():
-            send_block(d).wait_recv()
-            both_ways(functools.partial(halo, d), "start")
-
-        @pl.when(d == GROUPS)
-        def _():
+            send_block(wave, d).wait_recv()
+            both_ways(functools.partial(halo, wave, d), "start")
+
+        @pl.when(d >= LAG)
+        def _():
+            arrived(functools.partial(halo, wave, d - LAG))
+            chunk(wave, d - LAG)
+
+        return carry
+
+    for wave in range(WAVES):
+        lax.fori_loop(1, GROUPS + LAG, functools.partial(step, wave), 0)
+        if wave == WAVES - 1:
             both_ways(perm_halo, "start")
-
-        @pl.when(d >= LAG)
-        def _():
-            arrived(functools.partial(halo, d - LAG))
-            chunk(d - LAG)
-
-        return carry
-
-    lax.fori_loop(1, GROUPS + LAG, step, 0)
-
-    for layer in range(LAYERS):
-        half = OWN * LANES
+        part = LAYERS * STEP * LANES
         prod = jnp.dot(
             w_mat[...],
-            m_buf[:, layer * half : (layer + 1) * half],
+            m_buf[:, wave * part : (wave + 1) * part],
             preferred_element_type=F32,
         )
         prod = prod[:WIDE] + prod[WIDE:]
-        for r in range(OWN):
-            for go in range(GROUPS):
-                r_out[go, layer, r * PAD : (r + 1) * PAD, :] = prod[
-                    go * PAD : (go + 1) * PAD, r * LANES : (r + 1) * LANES
-                ]
+        for layer in range(LAYERS):
+            for r in range(STEP):
+                at = (layer * STEP + r) * LANES
+                for go in range(GROUPS):
+                    r_out[go, wave, layer, r * PAD : (r + 1) * PAD, :] = prod[
+                        go * PAD : (go + 1) * PAD, at : at + LANES
+                    ]
         for d in range(1, GROUPS):
-            send_back(d, layer).start()
-    ret[:, pl.ds(pl.multiple_of(m * OWN * PAD, OWN * PAD), OWN * PAD), :] = r_out[m]
+            send_back(wave, d).start()
+        ret[:, ret_rows(wave), :] = r_out[m, wave]
 
     own_cols = pl.ds(pl.multiple_of(2 * WIDE * m, 2 * WIDE), WIDE)
     own_rows = w_mat[mode_rows(m), own_cols].astype(F32) + w_mat[
@@ -388,19 +398,20 @@
     out_b.start()
     out_i.start()
 
+    for wave in range(WAVES):
+        for d in range(1, GROUPS):
+            send_back(wave, d).wait_recv()
     for layer in range(LAYERS):
-        for d in range(1, GROUPS):
-            send_back(d, layer).wait_recv()
         lax.fori_loop(0, LOCAL, functools.partial(finish, layer), 0)
     out_a = pltpu.make_async_copy(oa_v, out_a_hbm, out_sem.at[2])
     out_a.start()
 
-    for d in range(1, GROUPS):
-        send_block(d).wait_send()
-        for layer in range(LAYERS):
-            send_back(d, layer).wait_send()
-    for d in range(GROUPS):
-        both_ways(functools.partial(halo, d), "wait_send")
+    for wave in range(WAVES):
+        for d in range(1, GROUPS):
+            send_block(wave, d).wait_send()
+            send_back(wave, d).wait_send()
+        for d in range(GROUPS):
+            both_ways(functools.partial(halo, wave, d), "wait_send")
     both_ways(perm_halo, "wait_send")
     both_ways(strip, "wait_send")
     out_b.wait()
@@ -426,7 +437,7 @@
                 pltpu.VMEM((ENTRIES,), F32),
                 pltpu.VMEM((LAYERS, ROWS + 2, PAD, LANES), F32),
                 pltpu.VMEM((LAYERS + 2, OWN + 2, WIDE, LANES), F32),
-                pltpu.VMEM((GROUPS, LAYERS, OWN * PAD, LANES), F32),
+                pltpu.VMEM((GROUPS, WAVES, LAYERS, STEP * PAD, LANES), F32),
                 pltpu.VMEM((LAYERS, ROWS * PAD, LANES), F32),
                 pltpu.VMEM((2 * WIDE, GROUPS * 2 * WIDE), BF16),
                 pltpu.VMEM((2 * WIDE, ENTRIES), BF16),
@@ -442,9 +453,9 @@
                 pltpu.SemaphoreType.DMA((5,)),
                 pltpu.SemaphoreType.DMA((3,)),
             ]
-            + [pltpu.SemaphoreType.DMA((GROUPS,))] * 6
+            + [pltpu.SemaphoreType.DMA((WAVES, GROUPS))] * 6
             + [pltpu.SemaphoreType.DMA((2,))] * 4
-            + [pltpu.SemaphoreType.DMA((GROUPS, LAYERS))] * 2,
+            + [pltpu.SemaphoreType.DMA((WAVES, GROUPS))] * 2,
             compiler_params=pltpu.CompilerParams(
                 collective_id=0, has_side_effects=True, vmem_limit_bytes=60 * 1024 * 1024
             ),

time: 39.8 us -> 47.4 us (1.19)
  the two profiles are of different devices: /device:TPU:71 before, /device:TPU:103 now
where the time goes in v4:
time: 47.4 us; the launch traced here: 47.3 us
  Pallas kernels  44.3 us (93%)
  other arithmetic  2.35 us (5%)
  between operations  0.64 us (1%)
    pallas_call x1, Pallas kernels, on_device(): pl.pallas_call(functools.partial(kernel, space_count), out_shape=[jax.Sha...  44.3 us
    sub x1, other arithmetic, on_device(): relaxed = base - applied * inv  2.35 us

profile of v4, /device:TPU:103, one launch (start us, length us, event | category | flops | bytes accessed | tf_op | source)
XLA Modules:
  0.0 47.3 jit_solution(8624699141594225183)
XLA Ops:
  0.6 44.3 %shard_map.68 = (f32[960,128]{1,0:T(8,128)}, f32[960,128]{1,0:T(8,128)}, f32[960,128]{1,0:T(8,128)}) custom-call(f32[960,128]{1,0:T(8,128)} %bitcast.6, f32[960,128]{1,0:T(8,128)} %bitcast.7, f32[8,2,32,128]{3,2,1,0:T(8,128)} %a_hbm.1, s32[3,2880]{1,0:T(4,128)} %tri_hbm.1, f32[2880]{0:T(1024)} %cf_hbm.1), custom_call_target="tpu_custom_call" | custom-call | tf_op jit(solution)/shard_map/pallas_call | solution.py:427
  44.9 2.3 %multiply_subtract_fusion = (f32[960,128]{1,0:T(8,128)}, f32[960,128]{1,0:T(8,128)}) fusion(f32[960,128]{1,0:T(8,128)} %get-tuple-element.6, f32[960,128]{1,0:T(8,128)} %get-tuple-element.7, f32[960,128]{1,0:T(8,128)} %get-tuple-element.5), kind=kLoop, calls=%fused_computation | loop fusion | flops 368640 | bytes 2457600 | tf_op jit(solution)/shard_map/sub | solution.py:470

commit v5 on v3

--- a/solution.py
+++ b/solution.py
@@ -16,7 +16,8 @@
 LANES = 128
 OWN = ROWS // GROUPS
 ENTRIES = 2880
-LAG = 4
+HALVES = 2
+QUAD = GROUPS // HALVES
 EDGE = 8
 DATA = slice(EDGE, EDGE + ROWS)
 WIDE = GROUPS * PAD
@@ -77,11 +78,13 @@
     has_dn = s > 0
     has_up = s < space_count - 1
 
+    half_of = m // QUAD
+
     def peer_to(d):
-        return lax.rem(m + d, GROUPS)
+        return lax.rem(half_of + d // QUAD, HALVES) * QUAD + lax.rem(m + d, QUAD)
 
     def peer_from(d):
-        return lax.rem(m + GROUPS - d, GROUPS)
+        return lax.rem(half_of + d // QUAD, HALVES) * QUAD + lax.rem(m + GROUPS - d, QUAD)
 
     def mode_rows(g):
         return pl.ds(pl.multiple_of(g * PAD, PAD), PAD)
@@ -132,14 +135,15 @@
             device_id_type=MESH,
         )
 
-    def halo(d, up):
-        rows = mode_rows(peer_from(d))
+    def halo(part, up):
+        first = lax.rem(half_of + part, HALVES) * QUAD * PAD
+        rows = pl.ds(pl.multiple_of(first, QUAD * PAD), QUAD * PAD)
         sems = (high_send, high_recv) if up else (low_send, low_recv)
         return pltpu.make_async_remote_copy(
             src_ref=q.at[2 if up else 1, 1 : OWN + 1, rows, :],
             dst_ref=q.at[0 if up else 3, 1 : OWN + 1, rows, :],
-            send_sem=sems[0].at[d],
-            recv_sem=sems[1].at[d],
+            send_sem=sems[0].at[part],
+            recv_sem=sems[1].at[part],
             device_id=(m, s + 1 if up else s - 1),
             device_id_type=MESH,
         )
@@ -164,13 +168,13 @@
             device_id_type=MESH,
         )
 
-    def send_back(d, layer):
+    def send_back(d):
         g = peer_to(d)
         return pltpu.make_async_remote_copy(
-            src_ref=r_out.at[g, layer],
-            dst_ref=ret.at[layer, pl.ds(pl.multiple_of(m * OWN * PAD, OWN * PAD), OWN * PAD), :],
-            send_sem=ret_send.at[d, layer],
-            recv_sem=ret_recv.at[d, layer],
+            src_ref=r_out.at[g],
+            dst_ref=ret.at[:, pl.ds(pl.multiple_of(m * OWN * PAD, OWN * PAD), OWN * PAD), :],
+            send_sem=ret_send.at[d],
+            recv_sem=ret_recv.at[d],
             device_id=(g, s),
             device_id_type=MESH,
         )
@@ -208,7 +212,6 @@
     both_ways(strip, "start")
     for d in range(1, GROUPS):
         send_block(d).start()
-    both_ways(functools.partial(halo, 0), "start")
 
     @pl.when(jnp.logical_not(has_dn))
     def _():
@@ -253,8 +256,14 @@
                 w_mat[WIDE:, pl.ds(at, WIDE)] = lo
         return carry
 
-    lax.fori_loop(0, GROUPS // 2, table, 0)
-
+    def hand_on(part):
+        for d in range(max(part * QUAD, 1), (part + 1) * QUAD):
+            send_block(d).wait_recv()
+        both_ways(functools.partial(halo, part), "start")
+
+    lax.fori_loop(0, GROUPS // 4, table, 0)
+    hand_on(0)
+    lax.fori_loop(GROUPS // 4, GROUPS // 2, table, 0)
     arrived(strip)
     lane_ids = lax.broadcasted_iota(jnp.int32, (ROWS, LANES), 1)
 
@@ -269,6 +278,8 @@
         sides = (a_str[layer], a_str[layer + 2], a_y[0, layer], a_y[1, layer]) + beside(a)
         for f, side in enumerate(sides):
             w_f[f, layer] = a + side
+    hand_on(1)
+    both_ways(perm_halo, "start")
 
     def chunk(d):
         g = peer_from(d)
@@ -298,23 +309,12 @@
                         m_buf[pl.ds(to, PAD), at : at + LANES] = piece
 
     def step(d, carry):
-        @pl.when(d < GROUPS)
-        def _():
-            send_block(d).wait_recv()
-            both_ways(functools.partial(halo, d), "start")
-
-        @pl.when(d == GROUPS)
-        def _():
-            both_ways(perm_halo, "start")
-
-        @pl.when(d >= LAG)
-        def _():
-            arrived(functools.partial(halo, d - LAG))
-            chunk(d - LAG)
-
-        return carry
-
-    lax.fori_loop(1, GROUPS + LAG, step, 0)
+        chunk(d)
+        return carry
+
+    for part in range(HALVES):
+        arrived(functools.partial(halo, part))
+        lax.fori_loop(part * QUAD, (part + 1) * QUAD, step, 0)
 
     for layer in range(LAYERS):
         half = OWN * LANES
@@ -329,8 +329,8 @@
                 r_out[go, layer, r * PAD : (r + 1) * PAD, :] = prod[
                     go * PAD : (go + 1) * PAD, r * LANES : (r + 1) * LANES
                 ]
-        for d in range(1, GROUPS):
-            send_back(d, layer).start()
+    for d in range(1, GROUPS):
+        send_back(d).start()
     ret[:, pl.ds(pl.multiple_of(m * OWN * PAD, OWN * PAD), OWN * PAD), :] = r_out[m]
 
     own_cols = pl.ds(pl.multiple_of(2 * WIDE * m, 2 * WIDE), WIDE)
@@ -388,19 +388,18 @@
     out_b.start()
     out_i.start()
 
+    for d in range(1, GROUPS):
+        send_back(d).wait_recv()
     for layer in range(LAYERS):
-        for d in range(1, GROUPS):
-            send_back(d, layer).wait_recv()
         lax.fori_loop(0, LOCAL, functools.partial(finish, layer), 0)
     out_a = pltpu.make_async_copy(oa_v, out_a_hbm, out_sem.at[2])
     out_a.start()
 
     for d in range(1, GROUPS):
         send_block(d).wait_send()
-        for layer in range(LAYERS):
-            send_back(d, layer).wait_send()
-    for d in range(GROUPS):
-        both_ways(functools.partial(halo, d), "wait_send")
+        send_back(d).wait_send()
+    for part in range(HALVES):
+        both_ways(functools.partial(halo, part), "wait_send")
     both_ways(perm_halo, "wait_send")
     both_ways(strip, "wait_send")
     out_b.wait()
@@ -442,9 +441,10 @@
                 pltpu.SemaphoreType.DMA((5,)),
                 pltpu.SemaphoreType.DMA((3,)),
             ]
-            + [pltpu.SemaphoreType.DMA((GROUPS,))] * 6
+            + [pltpu.SemaphoreType.DMA((GROUPS,))] * 2
+            + [pltpu.SemaphoreType.DMA((HALVES,))] * 4
             + [pltpu.SemaphoreType.DMA((2,))] * 4
-            + [pltpu.SemaphoreType.DMA((GROUPS, LAYERS))] * 2,
+            + [pltpu.SemaphoreType.DMA((GROUPS,))] * 2,
             compiler_params=pltpu.CompilerParams(
                 collective_id=0, has_side_effects=True, vmem_limit_bytes=60 * 1024 * 1024
             ),

time: 39.8 us -> 39.4 us (0.990)
  the two profiles are of different devices: /device:TPU:71 before, /device:TPU:88 now
where the time goes in v5:
time: 39.4 us; the launch traced here: 38.7 us
  Pallas kernels  35.7 us (91%)
  other arithmetic  2.35 us (6%)
  between operations  0.64 us (2%)
    pallas_call x1, Pallas kernels, on_device(): pl.pallas_call(functools.partial(kernel, space_count), out_shape=[jax.Sha...  35.7 us
    sub x1, other arithmetic, on_device(): relaxed = base - applied * inv  2.35 us

profile of v5, /device:TPU:88, one launch (start us, length us, event | category | flops | bytes accessed | tf_op | source)
XLA Modules:
  0.0 38.7 jit_solution(2998517653034494643)
XLA Ops:
  0.6 35.7 %shard_map.68 = (f32[960,128]{1,0:T(8,128)}, f32[960,128]{1,0:T(8,128)}, f32[960,128]{1,0:T(8,128)}) custom-call(f32[960,128]{1,0:T(8,128)} %bitcast.6, f32[960,128]{1,0:T(8,128)} %bitcast.7, f32[8,2,32,128]{3,2,1,0:T(8,128)} %a_hbm.1, s32[3,2880]{1,0:T(4,128)} %tri_hbm.1, f32[2880]{0:T(1024)} %cf_hbm.1), custom_call_target="tpu_custom_call" | custom-call | tf_op jit(solution)/shard_map/pallas_call | solution.py:415
  36.3 2.3 %multiply_subtract_fusion = (f32[960,128]{1,0:T(8,128)}, f32[960,128]{1,0:T(8,128)}) fusion(f32[960,128]{1,0:T(8,128)} %get-tuple-element.6, f32[960,128]{1,0:T(8,128)} %get-tuple-element.7, f32[960,128]{1,0:T(8,128)} %get-tuple-element.5), kind=kLoop, calls=%fused_computation | loop fusion | flops 368640 | bytes 2457600 | tf_op jit(solution)/shard_map/sub | solution.py:459

commit v6 on v5

--- a/solution.py
+++ b/solution.py
@@ -18,6 +18,7 @@
 ENTRIES = 2880
 HALVES = 2
 QUAD = GROUPS // HALVES
+RUN = 8
 EDGE = 8
 DATA = slice(EDGE, EDGE + ROWS)
 WIDE = GROUPS * PAD
@@ -68,6 +69,9 @@
     high_recv,
     perm_send,
     perm_recv,
+    passing,
+    pass_send,
+    pass_recv,
     str_send,
     str_recv,
     ret_send,
@@ -77,6 +81,16 @@
     s = lax.axis_index("space")
     has_dn = s > 0
     has_up = s < space_count - 1
+    col = lax.rem(s, RUN)
+    is_first = col == 0
+    is_last = col == RUN - 1
+    is_end = jnp.logical_or(is_first, is_last)
+    run_up = s + RUN < space_count
+    run_dn = s >= RUN
+    steps_up = jnp.logical_and(is_last, has_up)
+    steps_dn = jnp.logical_and(is_first, has_dn)
+    passes_up = jnp.logical_and(is_first, run_up)
+    passes_dn = jnp.logical_and(is_last, run_dn)
 
     half_of = m // QUAD
 
@@ -100,6 +114,18 @@
     @pl.when(has_up)
     def _():
         pl.semaphore_signal(barrier, inc=1, device_id=(m, s + 1), device_id_type=MESH)
+
+    also = (
+        (is_first, s + RUN - 1),
+        (is_last, s - (RUN - 1)),
+        (jnp.logical_and(is_end, run_up), s + RUN),
+        (jnp.logical_and(is_end, run_dn), s - RUN),
+    )
+    for there, other in also:
+
+        @pl.when(there)
+        def _(other=other):
+            pl.semaphore_signal(barrier, inc=1, device_id=(m, other), device_id_type=MESH)
 
     load_p = pltpu.make_async_copy(p_hbm, p_v.at[0 : LOCAL * 64], in_sem.at[0])
     load_a = pltpu.make_async_copy(a_hbm, a_v.at[:, 1:3, DATA], in_sem.at[1])
@@ -135,18 +161,55 @@
             device_id_type=MESH,
         )
 
-    def halo(part, up):
+    def edge(part, up):
         first = lax.rem(half_of + part, HALVES) * QUAD * PAD
         rows = pl.ds(pl.multiple_of(first, QUAD * PAD), QUAD * PAD)
-        sems = (high_send, high_recv) if up else (low_send, low_recv)
+        send, recv = (high_send, high_recv) if up else (low_send, low_recv)
+        src = q.at[2 if up else 1, 1 : OWN + 1, rows, :]
+        dst = q.at[0 if up else 3, 1 : OWN + 1, rows, :]
+        return src, dst, send.at[part], recv.at[part]
+
+    def along(src, dst, send, recv, place):
         return pltpu.make_async_remote_copy(
-            src_ref=q.at[2 if up else 1, 1 : OWN + 1, rows, :],
-            dst_ref=q.at[0 if up else 3, 1 : OWN + 1, rows, :],
-            send_sem=sems[0].at[part],
-            recv_sem=sems[1].at[part],
-            device_id=(m, s + 1 if up else s - 1),
+            src_ref=src,
+            dst_ref=dst,
+            send_sem=send,
+            recv_sem=recv,
+            device_id=(m, place),
             device_id_type=MESH,
         )
+
+    def halo(part, up):
+        return along(*edge(part, up), s + 1 if up else s - 1)
+
+    def first_leg(up):
+        src, _, send, _ = edge(0, up)
+        place = s - (RUN - 1) if up else s + RUN - 1
+        return along(src, passing, send, pass_recv.at[0], place)
+
+    def second_leg(up):
+        _, dst, _, recv = edge(0, up)
+        return along(passing, dst, pass_send.at[0], recv, s + RUN if up else s - RUN)
+
+    def first_half(act):
+        for up, there, steps in ((True, has_up, steps_up), (False, has_dn, steps_dn)):
+
+            @pl.when(steps)
+            def _(up=up):
+                getattr(first_leg(up), act)()
+
+            @pl.when(jnp.logical_and(there, jnp.logical_not(steps)))
+            def _(up=up):
+                getattr(halo(0, up), act)()
+
+    def pass_on(act):
+        for up, passes in ((True, passes_up), (False, passes_dn)):
+
+            @pl.when(passes)
+            def _(up=up):
+                if act == "start":
+                    first_leg(up).wait_recv()
+                getattr(second_leg(up), act)()
 
     def perm_halo(up):
         return pltpu.make_async_remote_copy(
@@ -208,6 +271,8 @@
             a_y[1, layer, to, :] = a_v[k, layer + 1, pl.ds(EDGE + m * OWN + 1, OWN), :]
 
     neighbours = GROUPS - 1 + has_dn.astype(jnp.int32) + has_up.astype(jnp.int32)
+    for there, _ in also:
+        neighbours = neighbours + there.astype(jnp.int32)
     pl.semaphore_wait(barrier, neighbours)
     both_ways(strip, "start")
     for d in range(1, GROUPS):
@@ -259,7 +324,10 @@
     def hand_on(part):
         for d in range(max(part * QUAD, 1), (part + 1) * QUAD):
             send_block(d).wait_recv()
-        both_ways(functools.partial(halo, part), "start")
+        if part == 0:
+            first_half("start")
+        else:
+            both_ways(functools.partial(halo, part), "start")
 
     lax.fori_loop(0, GROUPS // 4, table, 0)
     hand_on(0)
@@ -278,8 +346,8 @@
         sides = (a_str[layer], a_str[layer + 2], a_y[0, layer], a_y[1, layer]) + beside(a)
         for f, side in enumerate(sides):
             w_f[f, layer] = a + side
+    pass_on("start")
     hand_on(1)
-    both_ways(perm_halo, "start")
 
     def chunk(d):
         g = peer_from(d)
@@ -314,6 +382,8 @@
 
     for part in range(HALVES):
         arrived(functools.partial(halo, part))
+        if part == HALVES - 1:
+            both_ways(perm_halo, "start")
         lax.fori_loop(part * QUAD, (part + 1) * QUAD, step, 0)
 
     for layer in range(LAYERS):
@@ -398,8 +468,9 @@
     for d in range(1, GROUPS):
         send_block(d).wait_send()
         send_back(d).wait_send()
-    for part in range(HALVES):
-        both_ways(functools.partial(halo, part), "wait_send")
+    first_half("wait_send")
+    pass_on("wait_send")
+    both_ways(functools.partial(halo, 1), "wait_send")
     both_ways(perm_halo, "wait_send")
     both_ways(strip, "wait_send")
     out_b.wait()
@@ -443,7 +514,10 @@
             ]
             + [pltpu.SemaphoreType.DMA((GROUPS,))] * 2
             + [pltpu.SemaphoreType.DMA((HALVES,))] * 4
-            + [pltpu.SemaphoreType.DMA((2,))] * 4
+            + [pltpu.SemaphoreType.DMA((2,))] * 2
+            + [pltpu.VMEM((OWN, QUAD * PAD, LANES), F32)]
+            + [pltpu.SemaphoreType.DMA((1,))] * 2
+            + [pltpu.SemaphoreType.DMA((2,))] * 2
             + [pltpu.SemaphoreType.DMA((GROUPS,))] * 2,
             compiler_params=pltpu.CompilerParams(
                 collective_id=0, has_side_effects=True, vmem_limit_bytes=60 * 1024 * 1024

time: 39.4 us -> 41.6 us (1.056)
  the two profiles are of different devices: /device:TPU:88 before, /device:TPU:7 now
where the time goes in v6:
time: 41.6 us; the launch traced here: 41.5 us
  Pallas kernels  38.5 us (93%)
  other arithmetic  2.35 us (6%)
  between operations  0.64 us (2%)
    pallas_call x1, Pallas kernels, on_device(): pl.pallas_call(functools.partial(kernel, space_count), out_shape=[jax.Sha...  38.5 us
    sub x1, other arithmetic, on_device(): relaxed = base - applied * inv  2.35 us

profile of v6, /device:TPU:7, one launch (start us, length us, event | category | flops | bytes accessed | tf_op | source)
XLA Modules:
  0.0 41.5 jit_solution(7717454203459464484)
XLA Ops:
  0.6 38.5 %shard_map.68 = (f32[960,128]{1,0:T(8,128)}, f32[960,128]{1,0:T(8,128)}, f32[960,128]{1,0:T(8,128)}) custom-call(f32[960,128]{1,0:T(8,128)} %bitcast.6, f32[960,128]{1,0:T(8,128)} %bitcast.7, f32[8,2,32,128]{3,2,1,0:T(8,128)} %a_hbm.1, s32[3,2880]{1,0:T(4,128)} %tri_hbm.1, f32[2880]{0:T(1024)} %cf_hbm.1), custom_call_target="tpu_custom_call" | custom-call | tf_op jit(solution)/shard_map/pallas_call | solution.py:486
  39.1 2.3 %multiply_subtract_fusion = (f32[960,128]{1,0:T(8,128)}, f32[960,128]{1,0:T(8,128)}) fusion(f32[960,128]{1,0:T(8,128)} %get-tuple-element.6, f32[960,128]{1,0:T(8,128)} %get-tuple-element.7, f32[960,128]{1,0:T(8,128)} %get-tuple-element.5), kind=kLoop, calls=%fused_computation | loop fusion | flops 368640 | bytes 2457600 | tf_op jit(solution)/shard_map/sub | solution.py:533

commit v7 on v5

--- a/solution.py
+++ b/solution.py
@@ -66,6 +66,10 @@
     low_recv,
     high_send,
     high_recv,
+    far_send,
+    far_recv,
+    row_send,
+    row_recv,
     perm_send,
     perm_recv,
     str_send,
@@ -86,6 +90,21 @@
     def peer_from(d):
         return lax.rem(half_of + d // QUAD, HALVES) * QUAD + lax.rem(m + GROUPS - d, QUAD)
 
+    def block_of(g):
+        return jnp.where(g < QUAD, g, GROUPS + QUAD - 1 - g)
+
+    block = block_of(m)
+    turned = half_of == 1
+    ahead = lax.rem(m, QUAD) < QUAD - 1
+    behind = lax.rem(m, QUAD) > 0
+    row_up, row_up_to = jnp.where(turned, 1, OWN), jnp.where(turned, OWN + 1, 0)
+    row_dn, row_dn_to = jnp.where(turned, OWN, 1), jnp.where(turned, 0, OWN + 1)
+
+    row_dn_to_far = jnp.where(turned, 0, OWN + 1)
+
+    def far_row(b):
+        return jnp.where(b == QUAD, QUAD * OWN, QUAD * OWN + 1)
+
     def mode_rows(g):
         return pl.ds(pl.multiple_of(g * PAD, PAD), PAD)
 
@@ -122,22 +141,84 @@
         return carry
 
     lax.fori_loop(0, ROWS, stage, 0)
-    q[1:3, :, mode_rows(m), :] = t[:, pl.ds(m * OWN, OWN + 2), :, :]
+    q[1:3, 1 : OWN + 1, mode_rows(m), :] = t[:, pl.ds(block * OWN + 1, OWN), :, :]
+
+    @pl.when(jnp.logical_not(ahead))
+    def _():
+        q[1:3, pl.ds(row_dn_to_far, 1), mode_rows(m), :] = t[:, pl.ds(far_row(block), 1), :, :]
+
+    @pl.when(jnp.logical_not(behind))
+    def _():
+        q[1:3, pl.ds(row_up_to, 1), :, :] = jnp.zeros((LAYERS, 1, WIDE, LANES), F32)
 
     def send_block(d):
         g = peer_to(d)
         return pltpu.make_async_remote_copy(
-            src_ref=t.at[:, pl.ds(g * OWN, OWN + 2)],
-            dst_ref=q.at[1:3, :, mode_rows(m), :],
+            src_ref=t.at[:, pl.ds(block_of(g) * OWN + 1, OWN)],
+            dst_ref=q.at[1:3, 1 : OWN + 1, mode_rows(m), :],
             send_sem=a2a_send.at[d],
             recv_sem=a2a_recv.at[d],
             device_id=(g, s),
             device_id_type=MESH,
         )
 
+    def send_far(d):
+        g = peer_to(d)
+        b = block_of(g)
+        to = jnp.where(b == QUAD, 0, OWN + 1)
+        return pltpu.make_async_remote_copy(
+            src_ref=t.at[:, pl.ds(far_row(b), 1)],
+            dst_ref=q.at[1:3, pl.ds(to, 1), mode_rows(m), :],
+            send_sem=far_send.at[d],
+            recv_sem=far_recv.at[d],
+            device_id=(g, s),
+            device_id_type=MESH,
+        )
+
+    def is_middle(d):
+        b = block_of(peer_to(d))
+        return jnp.logical_or(b == QUAD - 1, b == QUAD)
+
+    def halves(part):
+        first = lax.rem(half_of + part, HALVES) * QUAD * PAD
+        return pl.ds(pl.multiple_of(first, QUAD * PAD), QUAD * PAD)
+
+    def row_halo(part, up):
+        src, dst = (row_up, row_up_to) if up else (row_dn, row_dn_to)
+        return pltpu.make_async_remote_copy(
+            src_ref=q.at[1:3, pl.ds(src, 1), halves(part), :],
+            dst_ref=q.at[1:3, pl.ds(dst, 1), halves(part), :],
+            send_sem=row_send.at[part, 1 if up else 0],
+            recv_sem=row_recv.at[part, 1 if up else 0],
+            device_id=(m + 1 if up else m - 1, s),
+            device_id_type=MESH,
+        )
+
+    def rows_out(part, act):
+        @pl.when(ahead)
+        def _():
+            getattr(row_halo(part, True), act)()
+
+        @pl.when(behind)
+        def _():
+            getattr(row_halo(part, False), act)()
+
+    def rows_in(part):
+        @pl.when(behind)
+        def _():
+            row_halo(part, True).wait_recv()
+
+        @pl.when(ahead)
+        def _():
+            row_halo(part, False).wait_recv()
+
+        @pl.when(jnp.logical_not(ahead))
+        def _():
+            for d in range(max(part * QUAD, 1), (part + 1) * QUAD):
+                send_far(d).wait_recv()
+
     def halo(part, up):
-        first = lax.rem(half_of + part, HALVES) * QUAD * PAD
-        rows = pl.ds(pl.multiple_of(first, QUAD * PAD), QUAD * PAD)
+        rows = halves(part)
         sems = (high_send, high_recv) if up else (low_send, low_recv)
         return pltpu.make_async_remote_copy(
             src_ref=q.at[2 if up else 1, 1 : OWN + 1, rows, :],
@@ -168,11 +249,13 @@
             device_id_type=MESH,
         )
 
+    own_rows_back = pl.ds(pl.multiple_of(block * OWN * PAD, OWN * PAD), OWN * PAD)
+
     def send_back(d):
         g = peer_to(d)
         return pltpu.make_async_remote_copy(
             src_ref=r_out.at[g],
-            dst_ref=ret.at[:, pl.ds(pl.multiple_of(m * OWN * PAD, OWN * PAD), OWN * PAD), :],
+            dst_ref=ret.at[:, own_rows_back, :],
             send_sem=ret_send.at[d],
             recv_sem=ret_recv.at[d],
             device_id=(g, s),
@@ -203,15 +286,20 @@
         a_v[:, layer + 1, EDGE + ROWS :] = jnp.zeros((KA, EDGE, LANES), F32)
         for k in range(KA):
             to = slice(k * OWN, (k + 1) * OWN)
-            a_str[layer + 1, to, :] = a_v[k, layer + 1, pl.ds(EDGE + m * OWN, OWN), :]
-            a_y[0, layer, to, :] = a_v[k, layer + 1, pl.ds(EDGE + m * OWN - 1, OWN), :]
-            a_y[1, layer, to, :] = a_v[k, layer + 1, pl.ds(EDGE + m * OWN + 1, OWN), :]
+            a_str[layer + 1, to, :] = a_v[k, layer + 1, pl.ds(EDGE + block * OWN, OWN), :]
+            a_y[0, layer, to, :] = a_v[k, layer + 1, pl.ds(EDGE + block * OWN - 1, OWN), :]
+            a_y[1, layer, to, :] = a_v[k, layer + 1, pl.ds(EDGE + block * OWN + 1, OWN), :]
 
     neighbours = GROUPS - 1 + has_dn.astype(jnp.int32) + has_up.astype(jnp.int32)
     pl.semaphore_wait(barrier, neighbours)
     both_ways(strip, "start")
     for d in range(1, GROUPS):
         send_block(d).start()
+
+        @pl.when(is_middle(d))
+        def _(d=d):
+            send_far(d).start()
+
 
     @pl.when(jnp.logical_not(has_dn))
     def _():
@@ -260,6 +348,7 @@
         for d in range(max(part * QUAD, 1), (part + 1) * QUAD):
             send_block(d).wait_recv()
         both_ways(functools.partial(halo, part), "start")
+        rows_out(part, "start")
 
     lax.fori_loop(0, GROUPS // 4, table, 0)
     hand_on(0)
@@ -279,7 +368,6 @@
         for f, side in enumerate(sides):
             w_f[f, layer] = a + side
     hand_on(1)
-    both_ways(perm_halo, "start")
 
     def chunk(d):
         g = peer_from(d)
@@ -313,7 +401,10 @@
         return carry
 
     for part in range(HALVES):
+        rows_in(part)
         arrived(functools.partial(halo, part))
+        if part == HALVES - 1:
+            both_ways(perm_halo, "start")
         lax.fori_loop(part * QUAD, (part + 1) * QUAD, step, 0)
 
     for layer in range(LAYERS):
@@ -331,7 +422,7 @@
                 ]
     for d in range(1, GROUPS):
         send_back(d).start()
-    ret[:, pl.ds(pl.multiple_of(m * OWN * PAD, OWN * PAD), OWN * PAD), :] = r_out[m]
+    ret[:, own_rows_back, :] = r_out[m]
 
     own_cols = pl.ds(pl.multiple_of(2 * WIDE * m, 2 * WIDE), WIDE)
     own_rows = w_mat[mode_rows(m), own_cols].astype(F32) + w_mat[
@@ -398,8 +489,14 @@
     for d in range(1, GROUPS):
         send_block(d).wait_send()
         send_back(d).wait_send()
+
+        @pl.when(is_middle(d))
+        def _(d=d):
+            send_far(d).wait_send()
+
     for part in range(HALVES):
         both_ways(functools.partial(halo, part), "wait_send")
+        rows_out(part, "wait_send")
     both_ways(perm_halo, "wait_send")
     both_ways(strip, "wait_send")
     out_b.wait()
@@ -443,6 +540,8 @@
             ]
             + [pltpu.SemaphoreType.DMA((GROUPS,))] * 2
             + [pltpu.SemaphoreType.DMA((HALVES,))] * 4
+            + [pltpu.SemaphoreType.DMA((GROUPS,))] * 2
+            + [pltpu.SemaphoreType.DMA((HALVES, 2))] * 2
             + [pltpu.SemaphoreType.DMA((2,))] * 4
             + [pltpu.SemaphoreType.DMA((GROUPS,))] * 2,
             compiler_params=pltpu.CompilerParams(

time: 39.4 us -> 37.4 us (0.949); the launches traced: 38.7 us -> 37.2 us
  Pallas kernels: 35.7 us -> 34.2 us
    pallas_call x1, Pallas kernels: 35.7 us -> 34.2 us  [on_device(): pl.pallas_call(functools.partial(kernel, space_count), out_shape=[jax.Sha...]
where the time goes in v7:
time: 37.4 us; the launch traced here: 37.2 us
  Pallas kernels  34.2 us (91%)
  other arithmetic  2.35 us (6%)
  between operations  0.64 us (2%)
    pallas_call x1, Pallas kernels, on_device(): pl.pallas_call(functools.partial(kernel, space_count), out_shape=[jax.Sha...  34.2 us
    sub x1, other arithmetic, on_device(): relaxed = base - applied * inv  2.35 us

profile of v7, /device:TPU:88, one launch (start us, length us, event | category | flops | bytes accessed | tf_op | source)
XLA Modules:
  0.0 37.2 jit_solution(4085657376052153633)
XLA Ops:
  0.6 34.2 %shard_map.68 = (f32[960,128]{1,0:T(8,128)}, f32[960,128]{1,0:T(8,128)}, f32[960,128]{1,0:T(8,128)}) custom-call(f32[960,128]{1,0:T(8,128)} %bitcast.6, f32[960,128]{1,0:T(8,128)} %bitcast.7, f32[8,2,32,128]{3,2,1,0:T(8,128)} %a_hbm.1, s32[3,2880]{1,0:T(4,128)} %tri_hbm.1, f32[2880]{0:T(1024)} %cf_hbm.1), custom_call_target="tpu_custom_call" | custom-call | tf_op jit(solution)/shard_map/pallas_call | solution.py:512
  34.9 2.3 %multiply_subtract_fusion = (f32[960,128]{1,0:T(8,128)}, f32[960,128]{1,0:T(8,128)}) fusion(f32[960,128]{1,0:T(8,128)} %get-tuple-element.6, f32[960,128]{1,0:T(8,128)} %get-tuple-element.7, f32[960,128]{1,0:T(8,128)} %get-tuple-element.5), kind=kLoop, calls=%fused_computation | loop fusion | flops 368640 | bytes 2457600 | tf_op jit(solution)/shard_map/sub | solution.py:558

commit v8 on v7

--- a/solution.py
+++ b/solution.py
@@ -16,6 +16,7 @@
 LANES = 128
 OWN = ROWS // GROUPS
 ENTRIES = 2880
+DEPTH = 3072
 HALVES = 2
 QUAD = GROUPS // HALVES
 EDGE = 8
@@ -48,7 +49,9 @@
     r_out,
     ret,
     w_mat,
-    a_hot,
+    i_hot,
+    l_hot,
+    b_hot,
     m_buf,
     w_f,
     a_str,
@@ -319,29 +322,37 @@
     mode_j = tri_v[1:2, :]
     mode_k = tri_v[2:3, :]
     row_i = mode_i + ((mode_i * 274) >> 12)
-    col_jk = mode_j + 113 * ((mode_j * 274) >> 12) + PAD * mode_k
+    group_j = (mode_j * 274) >> 12
+    col_jk = mode_j - LOCAL * group_j + PAD * mode_k
     cf = cf_v[...].reshape(1, ENTRIES)
     cf_hi = cf.astype(BF16).astype(F32)
     cf_lo = cf - cf_hi
-    is_row = lax.broadcasted_iota(jnp.int32, (WIDE, ENTRIES), 0) == row_i
-    a_hot[0:WIDE, :] = jnp.where(is_row, cf_hi, 0.0).astype(BF16)
-    a_hot[WIDE:, :] = jnp.where(is_row, cf_lo, 0.0).astype(BF16)
+    ids = lax.broadcasted_iota(jnp.int32, (WIDE, ENTRIES), 0)
+    tail = ENTRIES // WIDE * WIDE
+    for hot in (i_hot, l_hot, b_hot):
+        hot[:, tail:] = jnp.zeros((hot.shape[0], DEPTH - tail), BF16)
+    i_hot[:, 0:ENTRIES] = jnp.where(ids == row_i, 1.0, 0.0).astype(BF16)
+    is_col = ids == col_jk
+    b_hot[0:WIDE, 0:ENTRIES] = jnp.where(is_col, cf_hi, 0.0).astype(BF16)
+    b_hot[WIDE:, 0:ENTRIES] = jnp.where(is_col, cf_lo, 0.0).astype(BF16)
 
     def table(c, carry):
-        cols = lax.broadcasted_iota(jnp.int32, (2 * WIDE, ENTRIES), 0) + c * (2 * WIDE)
-        b_hot = jnp.where(cols == col_jk, 1.0, 0.0).astype(BF16)
+        for part in range(QUAD):
+            mask = jnp.where(group_j == c * QUAD + part, 1.0, 0.0).astype(BF16)
+            rows = slice(part * WIDE, (part + 1) * WIDE)
+            l_hot[rows, 0:ENTRIES] = i_hot[:, 0:ENTRIES] * mask
         both = lax.dot_general(
-            a_hot[...], b_hot, (((1,), (1,)), ((), ())), preferred_element_type=F32
-        )
-        coupled = both[:WIDE] + both[WIDE:]
-        for part in range(2):
-            one = coupled[:, part * WIDE : (part + 1) * WIDE]
-            hi = one.astype(BF16)
-            lo = (one - hi.astype(F32)).astype(BF16)
+            l_hot[...], b_hot[...], (((1,), (1,)), ((), ())), preferred_element_type=F32
+        )
+        coupled = both[:, 0:WIDE] + both[:, WIDE:]
+        hi = coupled.astype(BF16)
+        lo = (coupled - hi.astype(F32)).astype(BF16)
+        for part in range(QUAD):
+            rows = slice(part * WIDE, (part + 1) * WIDE)
             for side in range(2):
-                at = pl.multiple_of(c * 4 * WIDE + (2 * part + side) * WIDE, WIDE)
-                w_mat[0:WIDE, pl.ds(at, WIDE)] = hi
-                w_mat[WIDE:, pl.ds(at, WIDE)] = lo
+                at = pl.multiple_of((c * QUAD + part) * 2 * WIDE + side * WIDE, WIDE)
+                w_mat[0:WIDE, pl.ds(at, WIDE)] = hi[rows]
+                w_mat[WIDE:, pl.ds(at, WIDE)] = lo[rows]
         return carry
 
     def hand_on(part):
@@ -350,9 +361,9 @@
         both_ways(functools.partial(halo, part), "start")
         rows_out(part, "start")
 
-    lax.fori_loop(0, GROUPS // 4, table, 0)
+    lax.fori_loop(0, 1, table, 0)
     hand_on(0)
-    lax.fori_loop(GROUPS // 4, GROUPS // 2, table, 0)
+    lax.fori_loop(1, 2, table, 0)
     arrived(strip)
     lane_ids = lax.broadcasted_iota(jnp.int32, (ROWS, LANES), 1)
 
@@ -525,7 +536,9 @@
                 pltpu.VMEM((GROUPS, LAYERS, OWN * PAD, LANES), F32),
                 pltpu.VMEM((LAYERS, ROWS * PAD, LANES), F32),
                 pltpu.VMEM((2 * WIDE, GROUPS * 2 * WIDE), BF16),
-                pltpu.VMEM((2 * WIDE, ENTRIES), BF16),
+                pltpu.VMEM((WIDE, DEPTH), BF16),
+                pltpu.VMEM((QUAD * WIDE, DEPTH), BF16),
+                pltpu.VMEM((2 * WIDE, DEPTH), BF16),
                 pltpu.VMEM((GROUPS * 2 * WIDE, LAYERS * OWN * LANES), BF16),
                 pltpu.VMEM((6, LAYERS, KA * OWN, LANES), F32),
                 pltpu.VMEM((LAYERS + 2, KA * OWN, LANES), F32),

time: 37.4 us -> 37.8 us (1.011)
  Pallas kernels: 34.2 us -> 34.7 us
    pallas_call x1, Pallas kernels: 34.2 us -> 34.7 us  [on_device(): pl.pallas_call(functools.partial(kernel, space_count), out_shape=[jax.Sha...]
where the time goes in v8:
time: 37.8 us; the launch traced here: 37.7 us
  Pallas kernels  34.7 us (92%)
  other arithmetic  2.35 us (6%)
  between operations  0.64 us (2%)
    pallas_call x1, Pallas kernels, on_device(): pl.pallas_call(functools.partial(kernel, space_count), out_shape=[jax.Sha...  34.7 us
    sub x1, other arithmetic, on_device(): relaxed = base - applied * inv  2.35 us

profile of v8, /device:TPU:88, one launch (start us, length us, event | category | flops | bytes accessed | tf_op | source)
XLA Modules:
  0.0 37.7 jit_solution(11414715155235174976)
XLA Ops:
  0.6 34.7 %shard_map.68 = (f32[960,128]{1,0:T(8,128)}, f32[960,128]{1,0:T(8,128)}, f32[960,128]{1,0:T(8,128)}) custom-call(f32[960,128]{1,0:T(8,128)} %bitcast.6, f32[960,128]{1,0:T(8,128)} %bitcast.7, f32[8,2,32,128]{3,2,1,0:T(8,128)} %a_hbm.1, s32[3,2880]{1,0:T(4,128)} %tri_hbm.1, f32[2880]{0:T(1024)} %cf_hbm.1), custom_call_target="tpu_custom_call" | custom-call | tf_op jit(solution)/shard_map/pallas_call | solution.py:523
  35.3 2.3 %multiply_subtract_fusion = (f32[960,128]{1,0:T(8,128)}, f32[960,128]{1,0:T(8,128)}) fusion(f32[960,128]{1,0:T(8,128)} %get-tuple-element.6, f32[960,128]{1,0:T(8,128)} %get-tuple-element.7, f32[960,128]{1,0:T(8,128)} %get-tuple-element.5), kind=kLoop, calls=%fused_computation | loop fusion | flops 368640 | bytes 2457600 | tf_op jit(solution)/shard_map/sub | solution.py:571

commit v9 on v7

--- a/solution.py
+++ b/solution.py
@@ -35,7 +35,7 @@
     a_hbm,
     tri_hbm,
     cf_hbm,
-    out_a_hbm,
+    ret,
     out_b_hbm,
     out_i_hbm,
     p_v,
@@ -46,7 +46,6 @@
     t,
     q,
     r_out,
-    ret,
     w_mat,
     a_hot,
     m_buf,
@@ -57,7 +56,6 @@
     cdb,
     inv_v,
     base_v,
-    oa_v,
     in_sem,
     out_sem,
     a2a_send,
@@ -422,7 +420,8 @@
                 ]
     for d in range(1, GROUPS):
         send_back(d).start()
-    ret[:, own_rows_back, :] = r_out[m]
+    keep = pltpu.make_async_copy(r_out.at[m], ret.at[:, own_rows_back, :], out_sem.at[2])
+    keep.start()
 
     own_cols = pl.ds(pl.multiple_of(2 * WIDE * m, 2 * WIDE), WIDE)
     own_rows = w_mat[mode_rows(m), own_cols].astype(F32) + w_mat[
@@ -467,24 +466,10 @@
 
     lax.fori_loop(0, LOCAL, scales, 0)
 
-    def finish(layer, j, carry):
-        for r8 in range(ROWS // 8):
-            got = ret[layer, pl.ds(r8 * 8 * PAD + j, 8, stride=PAD), :]
-            at = pl.ds(pl.multiple_of(j * 64 + layer * ROWS + r8 * 8, 8), 8)
-            oa_v[at, :] = got
-        return carry
-
     out_b = pltpu.make_async_copy(base_v, out_b_hbm, out_sem.at[0])
     out_i = pltpu.make_async_copy(inv_v, out_i_hbm, out_sem.at[1])
     out_b.start()
     out_i.start()
-
-    for d in range(1, GROUPS):
-        send_back(d).wait_recv()
-    for layer in range(LAYERS):
-        lax.fori_loop(0, LOCAL, functools.partial(finish, layer), 0)
-    out_a = pltpu.make_async_copy(oa_v, out_a_hbm, out_sem.at[2])
-    out_a.start()
 
     for d in range(1, GROUPS):
         send_block(d).wait_send()
@@ -501,7 +486,18 @@
     both_ways(strip, "wait_send")
     out_b.wait()
     out_i.wait()
-    out_a.wait()
+    keep.wait()
+    for d in range(1, GROUPS):
+        send_back(d).wait_recv()
+
+
+def finish(ret, base, inv, applied, relaxed):
+    for j in range(LOCAL):
+        for r8 in range(ROWS // 8):
+            rows = slice(r8 * 8, r8 * 8 + 8)
+            got = 0.5 * ret[0, pl.ds(r8 * 8 * PAD + j, 8, stride=PAD), :]
+            applied[j, 0, rows, :] = got
+            relaxed[j, 0, rows, :] = base[j, 0, rows, :] - got * inv[j, 0, rows, :]
 
 
 def solution(mesh):
@@ -509,9 +505,10 @@
     cells = (LOCAL * LAYERS * ROWS, LANES)
 
     def on_device(pressure, source, perm_modes, triples, coeffs):
-        doubled, base, inv = pl.pallas_call(
+        returned, base, inv = pl.pallas_call(
             functools.partial(kernel, space_count),
-            out_shape=[jax.ShapeDtypeStruct(cells, F32)] * 3,
+            out_shape=[jax.ShapeDtypeStruct((LAYERS, ROWS * PAD, LANES), F32)]
+            + [jax.ShapeDtypeStruct(cells, F32)] * 2,
             in_specs=[pl.BlockSpec(memory_space=pltpu.HBM)] * 5,
             out_specs=[pl.BlockSpec(memory_space=pl.ANY)] * 3,
             scratch_shapes=[
@@ -523,7 +520,6 @@
                 pltpu.VMEM((LAYERS, ROWS + 2, PAD, LANES), F32),
                 pltpu.VMEM((LAYERS + 2, OWN + 2, WIDE, LANES), F32),
                 pltpu.VMEM((GROUPS, LAYERS, OWN * PAD, LANES), F32),
-                pltpu.VMEM((LAYERS, ROWS * PAD, LANES), F32),
                 pltpu.VMEM((2 * WIDE, GROUPS * 2 * WIDE), BF16),
                 pltpu.VMEM((2 * WIDE, ENTRIES), BF16),
                 pltpu.VMEM((GROUPS * 2 * WIDE, LAYERS * OWN * LANES), BF16),
@@ -532,7 +528,6 @@
                 pltpu.VMEM((2, LAYERS, KA * OWN, LANES), F32),
                 pltpu.VMEM((KA, LAYERS, ROWS, LANES), F32),
                 pltpu.VMEM((KA, PAD, LANES), F32),
-                pltpu.VMEM(cells, F32),
                 pltpu.VMEM(cells, F32),
                 pltpu.VMEM(cells, F32),
                 pltpu.SemaphoreType.DMA((5,)),
@@ -554,9 +549,20 @@
             triples,
             coeffs,
         )
-        applied = 0.5 * doubled
-        relaxed = base - applied * inv
-        return applied.reshape(pressure.shape), relaxed.reshape(pressure.shape)
+        whole = (LOCAL, LAYERS, ROWS, LANES)
+        one_layer = pl.BlockSpec((LOCAL, 1, ROWS, LANES), lambda layer: (0, layer, 0, 0))
+        return pl.pallas_call(
+            finish,
+            grid=(LAYERS,),
+            out_shape=[jax.ShapeDtypeStruct(whole, F32)] * 2,
+            in_specs=[
+                pl.BlockSpec((1, ROWS * PAD, LANES), lambda layer: (layer, 0, 0)),
+                one_layer,
+                one_layer,
+            ],
+            out_specs=[one_layer] * 2,
+            compiler_params=pltpu.CompilerParams(vmem_limit_bytes=60 * 1024 * 1024),
+        )(returned, base.reshape(whole), inv.reshape(whole))
 
     return jax.shard_map(
         on_device,

time: 37.4 us -> 36.3 us (0.971)
  other arithmetic: 2.35 us -> 0 us
  Pallas kernels: 34.2 us -> 35.6 us
    sub x1 -> x0, other arithmetic: 2.35 us -> none  [on_device(): relaxed = base - applied * inv]
    pallas_call x0 -> x1, Pallas kernels: none -> 2.33 us  [on_device(): pl.pallas_call(finish, grid=(LAYERS,), out_shape=[jax.ShapeDtypeStruct(wh...]
    pallas_call x1, Pallas kernels: 34.2 us -> 33.2 us  [on_device(): pl.pallas_call(functools.partial(kernel, space_count), out_shape=[jax.Sha...]
where the time goes in v9:
time: 36.3 us; the launch traced here: 36.2 us
  Pallas kernels  35.6 us (98%)
  between operations  0.64 us (2%)
    pallas_call x1, Pallas kernels, on_device(): pl.pallas_call(functools.partial(kernel, space_count), out_shape=[jax.Sha...  33.2 us
    pallas_call x1, Pallas kernels, on_device(): pl.pallas_call(finish, grid=(LAYERS,), out_shape=[jax.ShapeDtypeStruct(wh...  2.33 us

profile of v9, /device:TPU:88, one launch (start us, length us, event | category | flops | bytes accessed | tf_op | source)
XLA Modules:
  0.0 36.2 jit_solution(12238418685308709851)
XLA Ops:
  0.6 33.2 %shard_map.68 = (f32[2,512,128]{2,1,0:T(8,128)}, f32[960,128]{1,0:T(8,128)}, f32[960,128]{1,0:T(8,128)}) custom-call(f32[960,128]{1,0:T(8,128)} %bitcast.4, f32[960,128]{1,0:T(8,128)} %bitcast.5, f32[8,2,32,128]{3,2,1,0:T(8,128)} %a_hbm.1, s32[3,2880]{1,0:T(4,128)} %tri_hbm.1, f32[2880]{0:T(1024)} %cf_hbm.1), custom_call_target="tpu_custom_call" | custom-call | tf_op jit(solution)/shard_map/pallas_call | solution.py:508
  33.9 2.3 %shard_map.69 = (f32[15,2,32,128]{3,2,1,0:T(8,128)}, f32[15,2,32,128]{3,2,1,0:T(8,128)}) custom-call(f32[2,512,128]{2,1,0:T(8,128)} %get-tuple-element.5.ret, f32[15,2,32,128]{3,2,1,0:T(8,128)} %bitcast.6, f32[15,2,32,128]{3,2,1,0:T(8,128)} %bitcast.7), custom_call_target="tpu_custom_call" | custom-call | tf_op jit(solution)/shard_map/pallas_call | solution.py:554

commit v10 on v9

--- a/solution.py
+++ b/solution.py
@@ -74,6 +74,7 @@
     str_recv,
     ret_send,
     ret_recv,
+    keep_sem,
 ):
     m = lax.axis_index("modes")
     s = lax.axis_index("space")
@@ -249,13 +250,18 @@
 
     own_rows_back = pl.ds(pl.multiple_of(block * OWN * PAD, OWN * PAD), OWN * PAD)
 
-    def send_back(d):
+    def keep(layer):
+        return pltpu.make_async_copy(
+            r_out.at[m, layer], ret.at[layer, own_rows_back, :], keep_sem.at[layer]
+        )
+
+    def send_back(d, layer):
         g = peer_to(d)
         return pltpu.make_async_remote_copy(
-            src_ref=r_out.at[g],
-            dst_ref=ret.at[:, own_rows_back, :],
-            send_sem=ret_send.at[d],
-            recv_sem=ret_recv.at[d],
+            src_ref=r_out.at[g, layer],
+            dst_ref=ret.at[layer, own_rows_back, :],
+            send_sem=ret_send.at[layer, d],
+            recv_sem=ret_recv.at[layer, d],
             device_id=(g, s),
             device_id_type=MESH,
         )
@@ -367,61 +373,65 @@
             w_f[f, layer] = a + side
     hand_on(1)
 
-    def chunk(d):
+    first_layer = lax.rem(s + 1, 2)
+
+    def edge_arrived(part, layer):
+        @pl.when(jnp.logical_and(layer == 0, has_dn))
+        def _():
+            halo(part, True).wait_recv()
+
+        @pl.when(jnp.logical_and(layer == 1, has_up))
+        def _():
+            halo(part, False).wait_recv()
+
+    def chunk(layer, d, carry):
         g = peer_from(d)
         rows = mode_rows(g)
         lanes = lax.broadcasted_iota(jnp.int32, (PAD, LANES), 1)
-        for layer in range(LAYERS):
-            for r in range(OWN):
-                p = q[layer + 1, r + 1, rows, :]
-                diffs = (
-                    p - q[layer, r + 1, rows, :],
-                    p - q[layer + 2, r + 1, rows, :],
-                    p - q[layer + 1, r, rows, :],
-                    p - q[layer + 1, r + 2, rows, :],
-                    p - jnp.where(lanes > 0, pltpu.roll(p, 1, 1), 0.0),
-                    p - jnp.where(lanes < LANES - 1, pltpu.roll(p, LANES - 1, 1), 0.0),
-                )
-                at = (layer * OWN + r) * LANES
-                for k in range(KA):
-                    total = None
-                    for f in range(6):
-                        term = w_f[f, layer, k * OWN + r : k * OWN + r + 1, :] * diffs[f]
-                        total = term if total is None else total + term
-                    hi = total.astype(BF16)
-                    lo = (total - hi.astype(F32)).astype(BF16)
-                    for part, piece in enumerate((hi, lo)):
-                        to = pl.multiple_of((2 * g + part) * WIDE + k * PAD, PAD)
-                        m_buf[pl.ds(to, PAD), at : at + LANES] = piece
-
-    def step(d, carry):
-        chunk(d)
+        for r in range(OWN):
+            p = q[layer + 1, r + 1, rows, :]
+            diffs = (
+                p - q[layer, r + 1, rows, :],
+                p - q[layer + 2, r + 1, rows, :],
+                p - q[layer + 1, r, rows, :],
+                p - q[layer + 1, r + 2, rows, :],
+                p - jnp.where(lanes > 0, pltpu.roll(p, 1, 1), 0.0),
+                p - jnp.where(lanes < LANES - 1, pltpu.roll(p, LANES - 1, 1), 0.0),
+            )
+            for k in range(KA):
+                total = None
+                for f in range(6):
+                    term = w_f[f, layer, k * OWN + r : k * OWN + r + 1, :] * diffs[f]
+                    total = term if total is None else total + term
+                hi = total.astype(BF16)
+                lo = (total - hi.astype(F32)).astype(BF16)
+                for part, piece in enumerate((hi, lo)):
+                    to = pl.multiple_of((2 * g + part) * WIDE + k * PAD, PAD)
+                    m_buf[layer, pl.ds(to, PAD), r * LANES : (r + 1) * LANES] = piece
         return carry
 
     for part in range(HALVES):
         rows_in(part)
-        arrived(functools.partial(halo, part))
-        if part == HALVES - 1:
-            both_ways(perm_halo, "start")
-        lax.fori_loop(part * QUAD, (part + 1) * QUAD, step, 0)
-
-    for layer in range(LAYERS):
-        half = OWN * LANES
-        prod = jnp.dot(
-            w_mat[...],
-            m_buf[:, layer * half : (layer + 1) * half],
-            preferred_element_type=F32,
-        )
-        prod = prod[:WIDE] + prod[WIDE:]
-        for r in range(OWN):
-            for go in range(GROUPS):
-                r_out[go, layer, r * PAD : (r + 1) * PAD, :] = prod[
-                    go * PAD : (go + 1) * PAD, r * LANES : (r + 1) * LANES
-                ]
-    for d in range(1, GROUPS):
-        send_back(d).start()
-    keep = pltpu.make_async_copy(r_out.at[m], ret.at[:, own_rows_back, :], out_sem.at[2])
-    keep.start()
+        depth = QUAD * 2 * WIDE
+        half_first = lax.rem(half_of + part, HALVES) * depth
+        deep = pl.ds(pl.multiple_of(half_first, depth), depth)
+        for turn in range(LAYERS):
+            layer = lax.rem(first_layer + turn, LAYERS)
+            edge_arrived(part, layer)
+            if part == HALVES - 1 and turn == LAYERS - 1:
+                both_ways(perm_halo, "start")
+            lax.fori_loop(part * QUAD, (part + 1) * QUAD, functools.partial(chunk, layer), 0)
+            prod = jnp.dot(w_mat[:, deep], m_buf[layer, deep, :], preferred_element_type=F32)
+            prod = prod[:WIDE] + prod[WIDE:]
+            for r in range(OWN):
+                for go in range(GROUPS):
+                    to = (go, layer, slice(r * PAD, (r + 1) * PAD))
+                    piece = prod[go * PAD : (go + 1) * PAD, r * LANES : (r + 1) * LANES]
+                    r_out[to] = piece if part == 0 else r_out[to] + piece
+            if part == HALVES - 1:
+                for d in range(1, GROUPS):
+                    send_back(d, layer).start()
+                keep(layer).start()
 
     own_cols = pl.ds(pl.multiple_of(2 * WIDE * m, 2 * WIDE), WIDE)
     own_rows = w_mat[mode_rows(m), own_cols].astype(F32) + w_mat[
@@ -473,7 +483,8 @@
 
     for d in range(1, GROUPS):
         send_block(d).wait_send()
-        send_back(d).wait_send()
+        for layer in range(LAYERS):
+            send_back(d, layer).wait_send()
 
         @pl.when(is_middle(d))
         def _(d=d):
@@ -486,9 +497,10 @@
     both_ways(strip, "wait_send")
     out_b.wait()
     out_i.wait()
-    keep.wait()
-    for d in range(1, GROUPS):
-        send_back(d).wait_recv()
+    for layer in range(LAYERS):
+        keep(layer).wait()
+        for d in range(1, GROUPS):
+            send_back(d, layer).wait_recv()
 
 
 def finish(ret, base, inv, applied, relaxed):
@@ -522,7 +534,7 @@
                 pltpu.VMEM((GROUPS, LAYERS, OWN * PAD, LANES), F32),
                 pltpu.VMEM((2 * WIDE, GROUPS * 2 * WIDE), BF16),
                 pltpu.VMEM((2 * WIDE, ENTRIES), BF16),
-                pltpu.VMEM((GROUPS * 2 * WIDE, LAYERS * OWN * LANES), BF16),
+                pltpu.VMEM((LAYERS, GROUPS * 2 * WIDE, OWN * LANES), BF16),
                 pltpu.VMEM((6, LAYERS, KA * OWN, LANES), F32),
                 pltpu.VMEM((LAYERS + 2, KA * OWN, LANES), F32),
                 pltpu.VMEM((2, LAYERS, KA * OWN, LANES), F32),
@@ -531,14 +543,15 @@
                 pltpu.VMEM(cells, F32),
                 pltpu.VMEM(cells, F32),
                 pltpu.SemaphoreType.DMA((5,)),
-                pltpu.SemaphoreType.DMA((3,)),
+                pltpu.SemaphoreType.DMA((2,)),
             ]
             + [pltpu.SemaphoreType.DMA((GROUPS,))] * 2
             + [pltpu.SemaphoreType.DMA((HALVES,))] * 4
             + [pltpu.SemaphoreType.DMA((GROUPS,))] * 2
             + [pltpu.SemaphoreType.DMA((HALVES, 2))] * 2
             + [pltpu.SemaphoreType.DMA((2,))] * 4
-            + [pltpu.SemaphoreType.DMA((GROUPS,))] * 2,
+            + [pltpu.SemaphoreType.DMA((LAYERS, GROUPS))] * 2
+            + [pltpu.SemaphoreType.DMA((LAYERS,))],
             compiler_params=pltpu.CompilerParams(
                 collective_id=0, has_side_effects=True, vmem_limit_bytes=60 * 1024 * 1024
             ),

time: 36.3 us -> 38.1 us (1.050)
  the two profiles are of different devices: /device:TPU:88 before, /device:TPU:39 now
where the time goes in v10:
time: 38.1 us; the launch traced here: 38 us
  Pallas kernels  37.4 us (98%)
  between operations  0.64 us (2%)
    pallas_call x1, Pallas kernels, on_device(): pl.pallas_call(functools.partial(kernel, space_count), out_shape=[jax.Sha...  35 us
    pallas_call x1, Pallas kernels, on_device(): pl.pallas_call(finish, grid=(LAYERS,), out_shape=[jax.ShapeDtypeStruct(wh...  2.33 us

profile of v10, /device:TPU:39, one launch (start us, length us, event | category | flops | bytes accessed | tf_op | source)
XLA Modules:
  0.0 38.0 jit_solution(6622606571505218268)
XLA Ops:
  0.6 35.0 %shard_map.68 = (f32[2,512,128]{2,1,0:T(8,128)}, f32[960,128]{1,0:T(8,128)}, f32[960,128]{1,0:T(8,128)}) custom-call(f32[960,128]{1,0:T(8,128)} %bitcast.4, f32[960,128]{1,0:T(8,128)} %bitcast.5, f32[8,2,32,128]{3,2,1,0:T(8,128)} %a_hbm.1, s32[3,2880]{1,0:T(4,128)} %tri_hbm.1, f32[2880]{0:T(1024)} %cf_hbm.1), custom_call_target="tpu_custom_call" | custom-call | tf_op jit(solution)/shard_map/pallas_call | solution.py:520
  35.7 2.3 %shard_map.69 = (f32[15,2,32,128]{3,2,1,0:T(8,128)}, f32[15,2,32,128]{3,2,1,0:T(8,128)}) custom-call(f32[2,512,128]{2,1,0:T(8,128)} %get-tuple-element.5.ret, f32[15,2,32,128]{3,2,1,0:T(8,128)} %bitcast.6, f32[15,2,32,128]{3,2,1,0:T(8,128)} %bitcast.7), custom_call_target="tpu_custom_call" | custom-call | tf_op jit(solution)/shard_map/pallas_call | solution.py:567

commit v11 on v10

--- a/solution.py
+++ b/solution.py
@@ -18,6 +18,7 @@
 ENTRIES = 2880
 HALVES = 2
 QUAD = GROUPS // HALVES
+RUN = 8
 EDGE = 8
 DATA = slice(EDGE, EDGE + ROWS)
 WIDE = GROUPS * PAD
@@ -75,11 +76,18 @@
     ret_send,
     ret_recv,
     keep_sem,
+    shared,
+    share_send,
+    share_recv,
 ):
     m = lax.axis_index("modes")
     s = lax.axis_index("space")
     has_dn = s > 0
     has_up = s < space_count - 1
+    steps_up = jnp.logical_and(has_up, lax.rem(s, RUN) == RUN - 1)
+    steps_dn = jnp.logical_and(has_dn, lax.rem(s, RUN) == 0)
+    near_up = jnp.logical_and(has_up, jnp.logical_not(steps_up))
+    near_dn = jnp.logical_and(has_dn, jnp.logical_not(steps_dn))
 
     half_of = m // QUAD
 
@@ -237,6 +245,55 @@
             device_id=(m, s + 1 if up else s - 1),
             device_id_type=MESH,
         )
+
+    def perm_out(act):
+        @pl.when(near_up)
+        def _():
+            getattr(perm_halo(True), act)()
+
+        @pl.when(near_dn)
+        def _():
+            getattr(perm_halo(False), act)()
+
+    def perm_in():
+        @pl.when(near_dn)
+        def _():
+            perm_halo(True).wait_recv()
+
+        @pl.when(near_up)
+        def _():
+            perm_halo(False).wait_recv()
+
+    def share(d, layer):
+        return pltpu.make_async_remote_copy(
+            src_ref=a_str.at[layer],
+            dst_ref=shared.at[block],
+            send_sem=share_send.at[d],
+            recv_sem=share_recv.at[d],
+            device_id=(peer_to(d), s),
+            device_id_type=MESH,
+        )
+
+    def share_all(act):
+        for there, layer in ((steps_dn, 0), (steps_up, 3)):
+
+            @pl.when(there)
+            def _(layer=layer):
+                for d in range(1, GROUPS):
+                    getattr(share(d, layer), act)()
+
+    def share_in():
+        for there, layer in ((steps_dn, 0), (steps_up, 3)):
+
+            @pl.when(there)
+            def _(layer=layer):
+                shared[pl.ds(block, 1)] = a_str[layer : layer + 1]
+                for d in range(1, GROUPS):
+                    share(d, layer).wait_recv()
+                for b in range(GROUPS):
+                    for k in range(KA):
+                        to = slice(EDGE + b * OWN, EDGE + (b + 1) * OWN)
+                        a_v[k, layer, to, :] = shared[b, k * OWN : (k + 1) * OWN, :]
 
     def strip(up):
         return pltpu.make_async_remote_copy(
@@ -372,6 +429,8 @@
         for f, side in enumerate(sides):
             w_f[f, layer] = a + side
     hand_on(1)
+    perm_out("start")
+    share_all("start")
 
     first_layer = lax.rem(s + 1, 2)
 
@@ -418,8 +477,6 @@
         for turn in range(LAYERS):
             layer = lax.rem(first_layer + turn, LAYERS)
             edge_arrived(part, layer)
-            if part == HALVES - 1 and turn == LAYERS - 1:
-                both_ways(perm_halo, "start")
             lax.fori_loop(part * QUAD, (part + 1) * QUAD, functools.partial(chunk, layer), 0)
             prod = jnp.dot(w_mat[:, deep], m_buf[layer, deep, :], preferred_element_type=F32)
             prod = prod[:WIDE] + prod[WIDE:]
@@ -443,7 +500,8 @@
         picked = jnp.where(lane == sub + k * PAD, own_rows, 0.0)
         cdb[k] = jnp.broadcast_to(jnp.sum(picked, axis=1, keepdims=True), (PAD, LANES))
 
-    arrived(perm_halo)
+    perm_in()
+    share_in()
 
     def diagonal(k, carry):
         for layer in range(LAYERS):
@@ -493,7 +551,8 @@
     for part in range(HALVES):
         both_ways(functools.partial(halo, part), "wait_send")
         rows_out(part, "wait_send")
-    both_ways(perm_halo, "wait_send")
+    perm_out("wait_send")
+    share_all("wait_send")
     both_ways(strip, "wait_send")
     out_b.wait()
     out_i.wait()
@@ -551,7 +610,9 @@
             + [pltpu.SemaphoreType.DMA((HALVES, 2))] * 2
             + [pltpu.SemaphoreType.DMA((2,))] * 4
             + [pltpu.SemaphoreType.DMA((LAYERS, GROUPS))] * 2
-            + [pltpu.SemaphoreType.DMA((LAYERS,))],
+            + [pltpu.SemaphoreType.DMA((LAYERS,))]
+            + [pltpu.VMEM((GROUPS, KA * OWN, LANES), F32)]
+            + [pltpu.SemaphoreType.DMA((GROUPS,))] * 2,
             compiler_params=pltpu.CompilerParams(
                 collective_id=0, has_side_effects=True, vmem_limit_bytes=60 * 1024 * 1024
             ),

time: 38.1 us -> 33.7 us (0.88)
  the two profiles are of different devices: /device:TPU:39 before, /device:TPU:88 now
where the time goes in v11:
time: 33.7 us; the launch traced here: 33.1 us
  Pallas kernels  32.4 us (96%)
  between operations  0.64 us (2%)
    pallas_call x1, Pallas kernels, on_device(): pl.pallas_call(functools.partial(kernel, space_count), out_shape=[jax.Sha...  30.1 us
    pallas_call x1, Pallas kernels, on_device(): pl.pallas_call(finish, grid=(LAYERS,), out_shape=[jax.ShapeDtypeStruct(wh...  2.33 us

profile of v11, /device:TPU:88, one launch (start us, length us, event | category | flops | bytes accessed | tf_op | source)
XLA Modules:
  0.0 33.1 jit_solution(11282670487905497326)
XLA Ops:
  0.6 30.1 %shard_map.68 = (f32[2,512,128]{2,1,0:T(8,128)}, f32[960,128]{1,0:T(8,128)}, f32[960,128]{1,0:T(8,128)}) custom-call(f32[960,128]{1,0:T(8,128)} %bitcast.4, f32[960,128]{1,0:T(8,128)} %bitcast.5, f32[8,2,32,128]{3,2,1,0:T(8,128)} %a_hbm.1, s32[3,2880]{1,0:T(4,128)} %tri_hbm.1, f32[2880]{0:T(1024)} %cf_hbm.1), custom_call_target="tpu_custom_call" | custom-call | tf_op jit(solution)/shard_map/pallas_call | solution.py:579
  30.7 2.3 %shard_map.69 = (f32[15,2,32,128]{3,2,1,0:T(8,128)}, f32[15,2,32,128]{3,2,1,0:T(8,128)}) custom-call(f32[2,512,128]{2,1,0:T(8,128)} %get-tuple-element.5.ret, f32[15,2,32,128]{3,2,1,0:T(8,128)} %bitcast.6, f32[15,2,32,128]{3,2,1,0:T(8,128)} %bitcast.7), custom_call_target="tpu_custom_call" | custom-call | tf_op jit(solution)/shard_map/pallas_call | solution.py:628

commit v12 on v11

--- a/solution.py
+++ b/solution.py
@@ -427,7 +427,9 @@
         a = a_str[layer + 1]
         sides = (a_str[layer], a_str[layer + 2], a_y[0, layer], a_y[1, layer]) + beside(a)
         for f, side in enumerate(sides):
-            w_f[f, layer] = a + side
+            w = a + side
+            for row in range(KA * OWN):
+                w_f[f, layer, row] = jnp.broadcast_to(w[row : row + 1], (8, LANES))
     hand_on(1)
     perm_out("start")
     share_all("start")
@@ -460,7 +462,8 @@
             for k in range(KA):
                 total = None
                 for f in range(6):
-                    term = w_f[f, layer, k * OWN + r : k * OWN + r + 1, :] * diffs[f]
+                    w = w_f[f, layer, k * OWN + r]
+                    term = jnp.concatenate([w, w], axis=0) * diffs[f]
                     total = term if total is None else total + term
                 hi = total.astype(BF16)
                 lo = (total - hi.astype(F32)).astype(BF16)
@@ -594,7 +597,7 @@
                 pltpu.VMEM((2 * WIDE, GROUPS * 2 * WIDE), BF16),
                 pltpu.VMEM((2 * WIDE, ENTRIES), BF16),
                 pltpu.VMEM((LAYERS, GROUPS * 2 * WIDE, OWN * LANES), BF16),
-                pltpu.VMEM((6, LAYERS, KA * OWN, LANES), F32),
+                pltpu.VMEM((6, LAYERS, KA * OWN, 8, LANES), F32),
                 pltpu.VMEM((LAYERS + 2, KA * OWN, LANES), F32),
                 pltpu.VMEM((2, LAYERS, KA * OWN, LANES), F32),
                 pltpu.VMEM((KA, LAYERS, ROWS, LANES), F32),

time: 33.7 us -> 33.7 us (level)
  no operation moved by 1% of the time
where the time goes in v12:
time: 33.7 us; the launch traced here: 33.3 us
  Pallas kernels  32.7 us (97%)
  between operations  0.64 us (2%)
    pallas_call x1, Pallas kernels, on_device(): pl.pallas_call(functools.partial(kernel, space_count), out_shape=[jax.Sha...  30.4 us
    pallas_call x1, Pallas kernels, on_device(): pl.pallas_call(finish, grid=(LAYERS,), out_shape=[jax.ShapeDtypeStruct(wh...  2.33 us

profile of v12, /device:TPU:88, one launch (start us, length us, event | category | flops | bytes accessed | tf_op | source)
XLA Modules:
  0.0 33.3 jit_solution(911252992603874944)
XLA Ops:
  0.6 30.4 %shard_map.68 = (f32[2,512,128]{2,1,0:T(8,128)}, f32[960,128]{1,0:T(8,128)}, f32[960,128]{1,0:T(8,128)}) custom-call(f32[960,128]{1,0:T(8,128)} %bitcast.4, f32[960,128]{1,0:T(8,128)} %bitcast.5, f32[8,2,32,128]{3,2,1,0:T(8,128)} %a_hbm.1, s32[3,2880]{1,0:T(4,128)} %tri_hbm.1, f32[2880]{0:T(1024)} %cf_hbm.1), custom_call_target="tpu_custom_call" | custom-call | tf_op jit(solution)/shard_map/pallas_call | solution.py:582
  31.0 2.3 %shard_map.69 = (f32[15,2,32,128]{3,2,1,0:T(8,128)}, f32[15,2,32,128]{3,2,1,0:T(8,128)}) custom-call(f32[2,512,128]{2,1,0:T(8,128)} %get-tuple-element.5.ret, f32[15,2,32,128]{3,2,1,0:T(8,128)} %bitcast.6, f32[15,2,32,128]{3,2,1,0:T(8,128)} %bitcast.7), custom_call_target="tpu_custom_call" | custom-call | tf_op jit(solution)/shard_map/pallas_call | solution.py:631

commit v13 on v11

--- a/solution.py
+++ b/solution.py
@@ -76,6 +76,8 @@
     ret_send,
     ret_recv,
     keep_sem,
+    c_buf,
+    swap_sem,
     shared,
     share_send,
     share_recv,
@@ -388,15 +390,31 @@
     a_hot[0:WIDE, :] = jnp.where(is_row, cf_hi, 0.0).astype(BF16)
     a_hot[WIDE:, :] = jnp.where(is_row, cf_lo, 0.0).astype(BF16)
 
-    def table(c, carry):
+    core = lax.rem(s, 2)
+    my_half = pl.ds(core * 2, 2)
+    swap = pltpu.make_async_remote_copy(
+        src_ref=c_buf.at[my_half],
+        dst_ref=c_buf.at[my_half],
+        send_sem=swap_sem.at[0],
+        recv_sem=swap_sem.at[1],
+        device_id=(m, s + 1 - 2 * core),
+        device_id_type=MESH,
+    )
+
+    def table(step, carry):
+        c = core * 2 + step
         cols = lax.broadcasted_iota(jnp.int32, (2 * WIDE, ENTRIES), 0) + c * (2 * WIDE)
         b_hot = jnp.where(cols == col_jk, 1.0, 0.0).astype(BF16)
         both = lax.dot_general(
             a_hot[...], b_hot, (((1,), (1,)), ((), ())), preferred_element_type=F32
         )
-        coupled = both[:WIDE] + both[WIDE:]
+        c_buf[c] = both[:WIDE] + both[WIDE:]
+        return carry
+
+    def place(first, step, carry):
+        c = first + step
         for part in range(2):
-            one = coupled[:, part * WIDE : (part + 1) * WIDE]
+            one = c_buf[c, :, part * WIDE : (part + 1) * WIDE]
             hi = one.astype(BF16)
             lo = (one - hi.astype(F32)).astype(BF16)
             for side in range(2):
@@ -411,9 +429,10 @@
         both_ways(functools.partial(halo, part), "start")
         rows_out(part, "start")
 
-    lax.fori_loop(0, GROUPS // 4, table, 0)
+    lax.fori_loop(0, 1, table, 0)
     hand_on(0)
-    lax.fori_loop(GROUPS // 4, GROUPS // 2, table, 0)
+    lax.fori_loop(1, 2, table, 0)
+    swap.start()
     arrived(strip)
     lane_ids = lax.broadcasted_iota(jnp.int32, (ROWS, LANES), 1)
 
@@ -431,6 +450,7 @@
     hand_on(1)
     perm_out("start")
     share_all("start")
+    lax.fori_loop(0, 2, functools.partial(place, core * 2), 0)
 
     first_layer = lax.rem(s + 1, 2)
 
@@ -478,6 +498,9 @@
             layer = lax.rem(first_layer + turn, LAYERS)
             edge_arrived(part, layer)
             lax.fori_loop(part * QUAD, (part + 1) * QUAD, functools.partial(chunk, layer), 0)
+            if part == 0 and turn == 0:
+                swap.wait_recv()
+                lax.fori_loop(0, 2, functools.partial(place, 2 - core * 2), 0)
             prod = jnp.dot(w_mat[:, deep], m_buf[layer, deep, :], preferred_element_type=F32)
             prod = prod[:WIDE] + prod[WIDE:]
             for r in range(OWN):
@@ -551,6 +574,7 @@
     for part in range(HALVES):
         both_ways(functools.partial(halo, part), "wait_send")
         rows_out(part, "wait_send")
+    swap.wait_send()
     perm_out("wait_send")
     share_all("wait_send")
     both_ways(strip, "wait_send")
@@ -611,6 +635,7 @@
             + [pltpu.SemaphoreType.DMA((2,))] * 4
             + [pltpu.SemaphoreType.DMA((LAYERS, GROUPS))] * 2
             + [pltpu.SemaphoreType.DMA((LAYERS,))]
+            + [pltpu.VMEM((GROUPS // 2, WIDE, 2 * WIDE), F32), pltpu.SemaphoreType.DMA((2,))]
             + [pltpu.VMEM((GROUPS, KA * OWN, LANES), F32)]
             + [pltpu.SemaphoreType.DMA((GROUPS,))] * 2,
             compiler_params=pltpu.CompilerParams(

time: 33.7 us -> 33.7 us (level)
  no operation moved by 1% of the time
where the time goes in v13:
time: 33.7 us; the launch traced here: 33.1 us
  Pallas kernels  32.5 us (96%)
  between operations  0.64 us (2%)
    pallas_call x1, Pallas kernels, on_device(): pl.pallas_call(functools.partial(kernel, space_count), out_shape=[jax.Sha...  30.1 us
    pallas_call x1, Pallas kernels, on_device(): pl.pallas_call(finish, grid=(LAYERS,), out_shape=[jax.ShapeDtypeStruct(wh...  2.33 us

profile of v13, /device:TPU:88, one launch (start us, length us, event | category | flops | bytes accessed | tf_op | source)
XLA Modules:
  0.0 33.1 jit_solution(7680646711702724640)
XLA Ops:
  0.6 30.1 %shard_map.68 = (f32[2,512,128]{2,1,0:T(8,128)}, f32[960,128]{1,0:T(8,128)}, f32[960,128]{1,0:T(8,128)}) custom-call(f32[960,128]{1,0:T(8,128)} %bitcast.4, f32[960,128]{1,0:T(8,128)} %bitcast.5, f32[8,2,32,128]{3,2,1,0:T(8,128)} %a_hbm.1, s32[3,2880]{1,0:T(4,128)} %tri_hbm.1, f32[2880]{0:T(1024)} %cf_hbm.1), custom_call_target="tpu_custom_call" | custom-call | tf_op jit(solution)/shard_map/pallas_call | solution.py:603
  30.8 2.3 %shard_map.69 = (f32[15,2,32,128]{3,2,1,0:T(8,128)}, f32[15,2,32,128]{3,2,1,0:T(8,128)}) custom-call(f32[2,512,128]{2,1,0:T(8,128)} %get-tuple-element.5.ret, f32[15,2,32,128]{3,2,1,0:T(8,128)} %bitcast.6, f32[15,2,32,128]{3,2,1,0:T(8,128)} %bitcast.7), custom_call_target="tpu_custom_call" | custom-call | tf_op jit(solution)/shard_map/pallas_call | solution.py:653

commit v14 on v11

--- a/solution.py
+++ b/solution.py
@@ -341,6 +341,16 @@
         def _():
             make(False).wait_recv()
 
+    neighbours = GROUPS - 1 + has_dn.astype(jnp.int32) + has_up.astype(jnp.int32)
+    pl.semaphore_wait(barrier, neighbours)
+    for d in range(1, GROUPS):
+        send_block(d).start()
+
+        @pl.when(is_middle(d))
+        def _(d=d):
+            send_far(d).start()
+
+
     load_a.wait()
     for layer in range(LAYERS):
         a_v[:, layer + 1, 0:EDGE] = jnp.zeros((KA, EDGE, LANES), F32)
@@ -350,17 +360,7 @@
             a_str[layer + 1, to, :] = a_v[k, layer + 1, pl.ds(EDGE + block * OWN, OWN), :]
             a_y[0, layer, to, :] = a_v[k, layer + 1, pl.ds(EDGE + block * OWN - 1, OWN), :]
             a_y[1, layer, to, :] = a_v[k, layer + 1, pl.ds(EDGE + block * OWN + 1, OWN), :]
-
-    neighbours = GROUPS - 1 + has_dn.astype(jnp.int32) + has_up.astype(jnp.int32)
-    pl.semaphore_wait(barrier, neighbours)
     both_ways(strip, "start")
-    for d in range(1, GROUPS):
-        send_block(d).start()
-
-        @pl.when(is_middle(d))
-        def _(d=d):
-            send_far(d).start()
-
 
     @pl.when(jnp.logical_not(has_dn))
     def _():

time: 33.7 us -> 33.7 us (level)
  Pallas kernels: 32.4 us -> 32.8 us
where the time goes in v14:
time: 33.7 us; the launch traced here: 33.4 us
  Pallas kernels  32.8 us (97%)
  between operations  0.64 us (2%)
    pallas_call x1, Pallas kernels, on_device(): pl.pallas_call(functools.partial(kernel, space_count), out_shape=[jax.Sha...  30.4 us
    pallas_call x1, Pallas kernels, on_device(): pl.pallas_call(finish, grid=(LAYERS,), out_shape=[jax.ShapeDtypeStruct(wh...  2.33 us

profile of v14, /device:TPU:88, one launch (start us, length us, event | category | flops | bytes accessed | tf_op | source)
XLA Modules:
  0.0 33.4 jit_solution(8905769312114032358)
XLA Ops:
  0.6 30.4 %shard_map.68 = (f32[2,512,128]{2,1,0:T(8,128)}, f32[960,128]{1,0:T(8,128)}, f32[960,128]{1,0:T(8,128)}) custom-call(f32[960,128]{1,0:T(8,128)} %bitcast.4, f32[960,128]{1,0:T(8,128)} %bitcast.5, f32[8,2,32,128]{3,2,1,0:T(8,128)} %a_hbm.1, s32[3,2880]{1,0:T(4,128)} %tri_hbm.1, f32[2880]{0:T(1024)} %cf_hbm.1), custom_call_target="tpu_custom_call" | custom-call | tf_op jit(solution)/shard_map/pallas_call | solution.py:579
  31.1 2.3 %shard_map.69 = (f32[15,2,32,128]{3,2,1,0:T(8,128)}, f32[15,2,32,128]{3,2,1,0:T(8,128)}) custom-call(f32[2,512,128]{2,1,0:T(8,128)} %get-tuple-element.5.ret, f32[15,2,32,128]{3,2,1,0:T(8,128)} %bitcast.6, f32[15,2,32,128]{3,2,1,0:T(8,128)} %bitcast.7), custom_call_target="tpu_custom_call" | custom-call | tf_op jit(solution)/shard_map/pallas_call | solution.py:628
